TPU v7x, 32 devices: a whole 2x2x4 slice. The times are simulated.
32 devices in a mesh: gx: 4 (over z), gy: 2 (over core), gz: 4 (over y, x).
Axes of the slice: x: 2, y: 2, z: 4, core: 2. Of those that a mesh axis runs over, the one named last changes fastest.
Arguments:
- noise: float32 [32, 64, 512], P('gx', 'gy', 'gz'), may hold values from -6 to 6
- kappa_sq: float32 [32, 64, 512], P('gx', 'gy', 'gz'), may hold values from 0.25 to 2
- cuts: int32 [6], replicated, may hold values from 0 to 24, as said below
- pressure_init: float32 [40, 64, 512], P('gx', 'gy', 'gz'), may hold values from -6 to 6
- source: float32 [40, 64, 512], P('gx', 'gy', 'gz'), may hold values from -24 to 24
Outputs:
- field: float32 [32, 64, 512], P('gx', 'gy', 'gz')
- pressure: float32 [40, 64, 512], P('gx', 'gy', 'gz')
Inputs may be any that keep to these rules, and one draw needn't show every extreme that they name: cuts[0] lies within 2 of 4; cuts[1] = 0 and cuts[5] = 24; cuts[i+1] lies within 2 of i * 6; in every draw some flow tile holds exactly 10 inset planes.
All inputs are finite; a program needn't handle non-finite values.
Results may differ from a plain program's by a relative error of at most 0.00002.
Values sent between devices are 32-bit elements; how exact they have to be, the bound alone decides.
A program may use at most 64 MiB of HBM per device.

v0:
```python
import jax
import jax.numpy as jnp
from jax import lax
from jax.sharding import PartitionSpec as P

SWEEPS = 8
JACOBI = 8


THETA = 7.125
DELTA = 6.875
LOG_GAIN = 2.0


def padded_2(value, sides, width):
    for axis, dim in sides:
        size, length = (lax.axis_size(axis), value.shape[dim])
        up = [(i, (i + 1) % size) for i in range(size - 1)]
        down = [(j, i) for i, j in up]
        last = lax.slice_in_dim(value, length - width, length, axis=dim)
        leading = lax.slice_in_dim(value, 0, width, axis=dim)
        before = lax.ppermute(last, axis, up)
        after = lax.ppermute(leading, axis, down)
        value = jnp.concatenate([before, value, after], axis=dim)
    return value


def from_behind(value, axis, by):
    size = lax.axis_size(axis)
    pairs = [(i, i + by) for i in range(size) if 0 <= i + by < size]
    return lax.ppermute(value, axis, pairs)


def sweep_weights(count):
    ratio_base = THETA / DELTA
    ratio_now = 1.0 / ratio_base
    weights = []
    for index in range(count):
        ratio_next = 1.0 / (2.0 * ratio_base - ratio_now)
        weights.append((ratio_next * ratio_now, 2.0 * ratio_next / DELTA))
        ratio_now = ratio_next
    return weights


def stencil(padded, kappa_core):
    core = padded[1:-1, 1:-1, 1:-1]
    beside = padded[2:, 1:-1, 1:-1] + padded[:-2, 1:-1, 1:-1]
    beside = beside + padded[1:-1, 2:, 1:-1] + padded[1:-1, :-2, 1:-1]
    beside = beside + padded[1:-1, 1:-1, 2:] + padded[1:-1, 1:-1, :-2]
    return (kappa_core + 6.0) * core - beside


def harmonic(own, other):
    return 2.0 * own * other / (own + other)


def local(noise, kappa_sq, cuts, pressure_init, source):
    cells_x, cells_y, cells_z = noise.shape
    count_x = lax.axis_size("gx")
    count_y = lax.axis_size("gy")
    count_z = lax.axis_size("gz")
    index_x = lax.axis_index("gx")
    index_y = lax.axis_index("gy")
    index_z = lax.axis_index("gz")
    weights = sweep_weights(SWEEPS)
    field = jnp.zeros_like(noise)
    resid = noise
    direction = noise / THETA
    for weight in weights:
        field = field + direction
        padded = padded_2(direction, (("gx", 0), ("gy", 1), ("gz", 2)), 1)
        resid = resid - stencil(padded, kappa_sq)
        direction = weight[0] * direction + weight[1] * resid
    perm_tile = jnp.exp(LOG_GAIN * field)
    flow_rows = pressure_init.shape[0]
    inset_planes = 3 * cells_x * count_x // 4
    rows = jnp.arange(flow_rows, dtype=jnp.int32)
    inset_begin = cuts[0]
    cut_here = lax.dynamic_index_in_dim(cuts, index_x + 1, 0, keepdims=False)
    cut_next = lax.dynamic_index_in_dim(cuts, index_x + 2, 0, keepdims=False)
    count_here = cut_next - cut_here
    live = rows < count_here
    wanted = inset_begin + cut_here + rows
    empty = jnp.zeros((flow_rows, cells_y, cells_z), jnp.float32)
    flow_mean = 3 * cells_x // 4
    jitter = (flow_mean - 2) // 2
    centre = cells_x * count_x // 8
    highest = (centre + 2 * jitter + flow_mean - 1) // cells_x
    lowest = (centre - 2 * jitter + (count_x - 1) * flow_mean) // cells_x - (count_x - 1)
    plane_ids = index_x * cells_x + jnp.arange(cells_x, dtype=jnp.int32) - inset_begin
    owner = jnp.sum((plane_ids[:, None] >= cuts[None, 2 : count_x + 1]).astype(jnp.int32), axis=1)
    owned = (plane_ids >= 0) & (plane_ids < inset_planes)
    source_dev = wanted // cells_x
    source_row = jnp.clip(wanted - source_dev * cells_x, 0, cells_x - 1)
    distance_of = source_dev - index_x
    moved = empty
    for distance in range(lowest, highest + 1):
        sending = jnp.where(((owner == index_x - distance) & owned)[:, None, None], perm_tile, 0.0)
        if distance == 0:
            arrived = sending
        else:
            arrived = from_behind(sending, "gx", -distance)
        picked = live & (distance_of == distance)
        moved = moved + jnp.where(picked[:, None, None], jnp.take(arrived, source_row, axis=0), 0.0)
    live_cells = live[:, None, None]
    perm_use = jnp.where(live_cells, moved, 1.0)
    pressure = jnp.where(live_cells, pressure_init, 0.0)
    last_row = rows == count_here - 1
    column_y = jnp.arange(cells_y, dtype=jnp.int32)
    column_z = jnp.arange(cells_z, dtype=jnp.int32)

    def neighbours(values):
        sides = padded_2(values, (("gy", 1), ("gz", 2)), 1)
        final = lax.dynamic_index_in_dim(values, count_here - 1, 0, keepdims=False)
        ends = padded_2(jnp.stack((values[0], final)), (("gx", 0),), 1)
        below = jnp.concatenate([ends[0][None], values[:-1]], axis=0)
        above = jnp.concatenate([values[1:], ends[3][None]], axis=0)
        above = jnp.where(last_row[:, None, None], ends[3][None], above)
        return (
            below,
            above,
            sides[:, :-2, 1:-1],
            sides[:, 2:, 1:-1],
            sides[:, 1:-1, :-2],
            sides[:, 1:-1, 2:],
        )

    borders = (
        ((index_x == 0) & (rows == 0))[:, None, None],
        ((index_x == count_x - 1) & last_row)[:, None, None],
        ((index_y == 0) & (column_y == 0))[None, :, None],
        ((index_y == count_y - 1) & (column_y == cells_y - 1))[None, :, None],
        ((index_z == 0) & (column_z == 0))[None, None, :],
        ((index_z == count_z - 1) & (column_z == cells_z - 1))[None, None, :],
    )
    perm_sides = neighbours(perm_use)
    coupling = [
        harmonic(perm_use, jnp.where(border, perm_use, other))
        for border, other in zip(borders, perm_sides)
    ]
    total = coupling[0] + coupling[1] + coupling[2] + coupling[3] + coupling[4] + coupling[5]
    for sweep in range(JACOBI):
        sides = neighbours(pressure)
        flux = source + coupling[0] * sides[0] + coupling[1] * sides[1] + coupling[2] * sides[2]
        flux = flux + coupling[3] * sides[3] + coupling[4] * sides[4] + coupling[5] * sides[5]
        pressure = jnp.where(live_cells, flux / total, 0.0)
    return (field, pressure)


def solution(mesh):
    placed = (
        P("gx", "gy", "gz"),
        P("gx", "gy", "gz"),
        P(),
        P("gx", "gy", "gz"),
        P("gx", "gy", "gz"),
    )
    return jax.shard_map(
        local,
        mesh=mesh,
        in_specs=placed,
        out_specs=(P("gx", "gy", "gz"), P("gx", "gy", "gz")),
        check_vma=False,
    )
```

profile of v0, /device:TPU:0, one launch (start us, length us, event | category | flops | bytes accessed | tf_op | source)
XLA Modules:
  0.0 383.8 jit_solution(5678670787053128555)
XLA Ops:
  1.6 4.9 %collective-permute-start.1 = (f32[1,32,128]{2,1,0:T(8,128)S(1)}, f32[1,32,128]{2,1,0:T(8,128)S(1)}, u32[]{:S(2)}, u32[]{:S(2)}) collective-permute-start(f32[1,32,128]{2,1,0:T(8,128)S(1)} %get-tuple-element.136), channel_id=1, source_target_pairs={{0,8},{8,16},{16,24},{1,9},{9,17},{17,25},{2,10},{10,18},{18,26},{... | collective-permute-start | bytes 49160 | tf_op jit(solution)/shard_map/ppermute | solution.py:22
  7.9 4.2 %collective-permute-done = f32[1,32,128]{2,1,0:T(8,128)S(1)} collective-permute-done((f32[1,32,128]{2,1,0:T(8,128)S(1)}, f32[1,32,128]{2,1,0:T(8,128)S(1)}, u32[]{:S(2)}, u32[]{:S(2)}) %collective-permute-start) | collective-permute-done | bytes 16416 | tf_op jit(solution)/shard_map/ppermute | solution.py:23
  18.0 4.6 %collective-permute-start.5 = (f32[10,34,1]{2,1,0:T(8,128)S(1)}, f32[10,34,1]{2,1,0:T(8,128)S(1)}, u32[]{:S(2)}, u32[]{:S(2)}) collective-permute-start(f32[10,34,1]{2,1,0:T(8,128)S(1)} %get-tuple-element.53), channel_id=1, source_target_pairs={{0,1},{1,2},{2,3},{4,5},{5,6},{6,7},{8,9},{9,10},{10,11},{12,13},{... | collective-permute-start | bytes 4088 | tf_op jit(solution)/shard_map/ppermute | solution.py:22
  32.0 4.2 %collective-permute-done.6 = f32[1,32,128]{2,1,0:T(8,128)S(1)} collective-permute-done((f32[1,32,128]{2,1,0:T(8,128)S(1)}, f32[1,32,128]{2,1,0:T(8,128)S(1)}, u32[]{:S(2)}, u32[]{:S(2)}) %collective-permute-start.6) | collective-permute-done | bytes 16416 | tf_op jit(solution)/shard_map/ppermute | solution.py:23
  42.1 5.3 %collective-permute-start.11 = (f32[10,34,1]{2,1,0:T(8,128)S(1)}, f32[10,34,1]{2,1,0:T(8,128)S(1)}, u32[]{:S(2)}, u32[]{:S(2)}) collective-permute-start(f32[10,34,1]{2,1,0:T(8,128)S(1)} %get-tuple-element.51), channel_id=1, source_target_pairs={{0,1},{1,2},{2,3},{4,5},{5,6},{6,7},{8,9},{9,10},{10,11},{12,13},{... | collective-permute-start | bytes 4088 | tf_op jit(solution)/shard_map/ppermute | solution.py:22
  57.1 4.2 %collective-permute-done.12 = f32[1,32,128]{2,1,0:T(8,128)S(1)} collective-permute-done((f32[1,32,128]{2,1,0:T(8,128)S(1)}, f32[1,32,128]{2,1,0:T(8,128)S(1)}, u32[]{:S(2)}, u32[]{:S(2)}) %collective-permute-start.12) | collective-permute-done | bytes 16416 | tf_op jit(solution)/shard_map/ppermute | solution.py:23
  67.2 5.9 %collective-permute-start.17 = (f32[10,34,1]{2,1,0:T(8,128)S(1)}, f32[10,34,1]{2,1,0:T(8,128)S(1)}, u32[]{:S(2)}, u32[]{:S(2)}) collective-permute-start(f32[10,34,1]{2,1,0:T(8,128)S(1)} %get-tuple-element.49), channel_id=1, source_target_pairs={{0,1},{1,2},{2,3},{4,5},{5,6},{6,7},{8,9},{9,10},{10,11},{12,13},{... | collective-permute-start | bytes 4088 | tf_op jit(solution)/shard_map/ppermute | solution.py:22
  81.3 4.2 %collective-permute-done.18 = f32[1,32,128]{2,1,0:T(8,128)S(1)} collective-permute-done((f32[1,32,128]{2,1,0:T(8,128)S(1)}, f32[1,32,128]{2,1,0:T(8,128)S(1)}, u32[]{:S(2)}, u32[]{:S(2)}) %collective-permute-start.18) | collective-permute-done | bytes 16416 | tf_op jit(solution)/shard_map/ppermute | solution.py:23
  91.4 5.9 %collective-permute-start.23 = (f32[10,34,1]{2,1,0:T(8,128)S(1)}, f32[10,34,1]{2,1,0:T(8,128)S(1)}, u32[]{:S(2)}, u32[]{:S(2)}) collective-permute-start(f32[10,34,1]{2,1,0:T(8,128)S(1)} %get-tuple-element.47), channel_id=1, source_target_pairs={{0,1},{1,2},{2,3},{4,5},{5,6},{6,7},{8,9},{9,10},{10,11},{12,13},{... | collective-permute-start | bytes 4088 | tf_op jit(solution)/shard_map/ppermute | solution.py:22
  105.5 4.2 %collective-permute-done.24 = f32[1,32,128]{2,1,0:T(8,128)S(1)} collective-permute-done((f32[1,32,128]{2,1,0:T(8,128)S(1)}, f32[1,32,128]{2,1,0:T(8,128)S(1)}, u32[]{:S(2)}, u32[]{:S(2)}) %collective-permute-start.24) | collective-permute-done | bytes 16416 | tf_op jit(solution)/shard_map/ppermute | solution.py:23
  117.1 5.9 %collective-permute-start.29 = (f32[10,34,1]{2,1,0:T(8,128)S(1)}, f32[10,34,1]{2,1,0:T(8,128)S(1)}, u32[]{:S(2)}, u32[]{:S(2)}) collective-permute-start(f32[10,34,1]{2,1,0:T(8,128)S(1)} %get-tuple-element.45), channel_id=1, source_target_pairs={{0,1},{1,2},{2,3},{4,5},{5,6},{6,7},{8,9},{9,10},{10,11},{12,13},{... | collective-permute-start | bytes 4088 | tf_op jit(solution)/shard_map/ppermute | solution.py:22
  131.9 4.2 %collective-permute-done.30 = f32[1,32,128]{2,1,0:T(8,128)S(1)} collective-permute-done((f32[1,32,128]{2,1,0:T(8,128)S(1)}, f32[1,32,128]{2,1,0:T(8,128)S(1)}, u32[]{:S(2)}, u32[]{:S(2)}) %collective-permute-start.30) | collective-permute-done | bytes 16416 | tf_op jit(solution)/shard_map/ppermute | solution.py:23
  141.9 5.9 %collective-permute-start.35 = (f32[10,34,1]{2,1,0:T(8,128)S(1)}, f32[10,34,1]{2,1,0:T(8,128)S(1)}, u32[]{:S(2)}, u32[]{:S(2)}) collective-permute-start(f32[10,34,1]{2,1,0:T(8,128)S(1)} %get-tuple-element.43), channel_id=1, source_target_pairs={{0,1},{1,2},{2,3},{4,5},{5,6},{6,7},{8,9},{9,10},{10,11},{12,13},{... | collective-permute-start | bytes 4088 | tf_op jit(solution)/shard_map/ppermute | solution.py:22
  156.1 4.2 %collective-permute-done.36 = f32[1,32,128]{2,1,0:T(8,128)S(1)} collective-permute-done((f32[1,32,128]{2,1,0:T(8,128)S(1)}, f32[1,32,128]{2,1,0:T(8,128)S(1)}, u32[]{:S(2)}, u32[]{:S(2)}) %collective-permute-start.36) | collective-permute-done | bytes 16416 | tf_op jit(solution)/shard_map/ppermute | solution.py:23
  166.1 5.9 %collective-permute-start.41 = (f32[10,34,1]{2,1,0:T(8,128)S(1)}, f32[10,34,1]{2,1,0:T(8,128)S(1)}, u32[]{:S(2)}, u32[]{:S(2)}) collective-permute-start(f32[10,34,1]{2,1,0:T(8,128)S(1)} %get-tuple-element.41), channel_id=1, source_target_pairs={{0,1},{1,2},{2,3},{4,5},{5,6},{6,7},{8,9},{9,10},{10,11},{12,13},{... | collective-permute-start | bytes 4088 | tf_op jit(solution)/shard_map/ppermute | solution.py:22
  195.5 5.3 %collective-permute-start.53 = (f32[10,34,1]{2,1,0:T(8,128)S(1)}, f32[10,34,1]{2,1,0:T(8,128)S(1)}, u32[]{:S(2)}, u32[]{:S(2)}) collective-permute-start(f32[10,34,1]{2,1,0:T(8,128)S(1)} %get-tuple-element.38), channel_id=1, source_target_pairs={{0,1},{1,2},{2,3},{4,5},{5,6},{6,7},{8,9},{9,10},{10,11},{12,13},{... | collective-permute-start | bytes 4088 | tf_op jit(solution)/shard_map/ppermute | solution.py:22
  204.7 4.5 %collective-permute-start.45 = (f32[1,32,128]{2,1,0:T(8,128)S(1)}, f32[1,32,128]{2,1,0:T(8,128)S(1)}, u32[]{:S(2)}, u32[]{:S(2)}) collective-permute-start(f32[1,32,128]{2,1,0:T(8,128)S(1)} %get-tuple-element.105), channel_id=1, source_target_pairs={{0,8},{8,16},{16,24},{1,9},{9,17},{17,25},{2,10},{10,18},{18,26},{... | collective-permute-start | bytes 49160 | tf_op jit(solution)/shard_map/ppermute | solution.py:22
  230.4 4.5 %collective-permute-start.56 = (f32[1,32,128]{2,1,0:T(8,128)S(1)}, f32[1,32,128]{2,1,0:T(8,128)S(1)}, u32[]{:S(2)}, u32[]{:S(2)}) collective-permute-start(f32[1,32,128]{2,1,0:T(8,128)S(1)} %get-tuple-element.93), channel_id=1, source_target_pairs={{0,8},{8,16},{16,24},{1,9},{9,17},{17,25},{2,10},{10,18},{18,26},{... | collective-permute-start | bytes 49160 | tf_op jit(solution)/shard_map/ppermute | solution.py:22
  235.1 4.4 %collective-permute-start.60 = (f32[10,34,1]{2,1,0:T(8,128)S(1)}, f32[10,34,1]{2,1,0:T(8,128)S(1)}, u32[]{:S(2)}, u32[]{:S(2)}) collective-permute-start(f32[10,34,1]{2,1,0:T(8,128)S(1)} %get-tuple-element.34), channel_id=1, source_target_pairs={{0,1},{1,2},{2,3},{4,5},{5,6},{6,7},{8,9},{9,10},{10,11},{12,13},{... | collective-permute-start | bytes 4088 | tf_op jit(solution)/shard_map/ppermute | solution.py:22
  244.5 6.3 %collective-permute-done.61 = f32[10,34,1]{2,1,0:T(8,128)S(1)} collective-permute-done((f32[10,34,1]{2,1,0:T(8,128)S(1)}, f32[10,34,1]{2,1,0:T(8,128)S(1)}, u32[]{:S(2)}, u32[]{:S(2)}) %collective-permute-start.61) | collective-permute-done | bytes 1392 | tf_op jit(solution)/shard_map/ppermute | solution.py:23
  255.7 4.5 %collective-permute-start.62 = (f32[1,32,128]{2,1,0:T(8,128)S(1)}, f32[1,32,128]{2,1,0:T(8,128)S(1)}, u32[]{:S(2)}, u32[]{:S(2)}) collective-permute-start(f32[1,32,128]{2,1,0:T(8,128)S(1)} %get-tuple-element.87), channel_id=1, source_target_pairs={{0,8},{8,16},{16,24},{1,9},{9,17},{17,25},{2,10},{10,18},{18,26},{... | collective-permute-start | bytes 49160 | tf_op jit(solution)/shard_map/ppermute | solution.py:22
  268.6 5.1 %collective-permute-done.67 = f32[10,34,1]{2,1,0:T(8,128)S(1)} collective-permute-done((f32[10,34,1]{2,1,0:T(8,128)S(1)}, f32[10,34,1]{2,1,0:T(8,128)S(1)}, u32[]{:S(2)}, u32[]{:S(2)}) %collective-permute-start.67) | collective-permute-done | bytes 1392 | tf_op jit(solution)/shard_map/ppermute | solution.py:23
  278.7 4.5 %collective-permute-start.68 = (f32[1,32,128]{2,1,0:T(8,128)S(1)}, f32[1,32,128]{2,1,0:T(8,128)S(1)}, u32[]{:S(2)}, u32[]{:S(2)}) collective-permute-start(f32[1,32,128]{2,1,0:T(8,128)S(1)} %get-tuple-element.81), channel_id=1, source_target_pairs={{0,8},{8,16},{16,24},{1,9},{9,17},{17,25},{2,10},{10,18},{18,26},{... | collective-permute-start | bytes 49160 | tf_op jit(solution)/shard_map/ppermute | solution.py:22
  290.3 5.1 %collective-permute-done.73 = f32[10,34,1]{2,1,0:T(8,128)S(1)} collective-permute-done((f32[10,34,1]{2,1,0:T(8,128)S(1)}, f32[10,34,1]{2,1,0:T(8,128)S(1)}, u32[]{:S(2)}, u32[]{:S(2)}) %collective-permute-start.73) | collective-permute-done | bytes 1392 | tf_op jit(solution)/shard_map/ppermute | solution.py:23
  300.4 4.5 %collective-permute-start.74 = (f32[1,32,128]{2,1,0:T(8,128)S(1)}, f32[1,32,128]{2,1,0:T(8,128)S(1)}, u32[]{:S(2)}, u32[]{:S(2)}) collective-permute-start(f32[1,32,128]{2,1,0:T(8,128)S(1)} %get-tuple-element.75), channel_id=1, source_target_pairs={{0,8},{8,16},{16,24},{1,9},{9,17},{17,25},{2,10},{10,18},{18,26},{... | collective-permute-start | bytes 49160 | tf_op jit(solution)/shard_map/ppermute | solution.py:22
  312.1 5.1 %collective-permute-done.79 = f32[10,34,1]{2,1,0:T(8,128)S(1)} collective-permute-done((f32[10,34,1]{2,1,0:T(8,128)S(1)}, f32[10,34,1]{2,1,0:T(8,128)S(1)}, u32[]{:S(2)}, u32[]{:S(2)}) %collective-permute-start.79) | collective-permute-done | bytes 1392 | tf_op jit(solution)/shard_map/ppermute | solution.py:23
  322.2 4.7 %collective-permute-start.80 = (f32[1,32,128]{2,1,0:T(8,128)S(1)}, f32[1,32,128]{2,1,0:T(8,128)S(1)}, u32[]{:S(2)}, u32[]{:S(2)}) collective-permute-start(f32[1,32,128]{2,1,0:T(8,128)S(1)} %get-tuple-element.69), channel_id=1, source_target_pairs={{0,8},{8,16},{16,24},{1,9},{9,17},{17,25},{2,10},{10,18},{18,26},{... | collective-permute-start | bytes 49160 | tf_op jit(solution)/shard_map/ppermute | solution.py:22
  334.0 5.1 %collective-permute-done.85 = f32[10,34,1]{2,1,0:T(8,128)S(1)} collective-permute-done((f32[10,34,1]{2,1,0:T(8,128)S(1)}, f32[10,34,1]{2,1,0:T(8,128)S(1)}, u32[]{:S(2)}, u32[]{:S(2)}) %collective-permute-start.85) | collective-permute-done | bytes 1392 | tf_op jit(solution)/shard_map/ppermute | solution.py:23
  344.1 4.5 %collective-permute-start.86 = (f32[1,32,128]{2,1,0:T(8,128)S(1)}, f32[1,32,128]{2,1,0:T(8,128)S(1)}, u32[]{:S(2)}, u32[]{:S(2)}) collective-permute-start(f32[1,32,128]{2,1,0:T(8,128)S(1)} %get-tuple-element.63), channel_id=1, source_target_pairs={{0,8},{8,16},{16,24},{1,9},{9,17},{17,25},{2,10},{10,18},{18,26},{... | collective-permute-start | bytes 49160 | tf_op jit(solution)/shard_map/ppermute | solution.py:22
  355.8 5.1 %collective-permute-done.91 = f32[10,34,1]{2,1,0:T(8,128)S(1)} collective-permute-done((f32[10,34,1]{2,1,0:T(8,128)S(1)}, f32[10,34,1]{2,1,0:T(8,128)S(1)}, u32[]{:S(2)}, u32[]{:S(2)}) %collective-permute-start.91) | collective-permute-done | bytes 1392 | tf_op jit(solution)/shard_map/ppermute | solution.py:23
  365.9 4.5 %collective-permute-start.92 = (f32[1,32,128]{2,1,0:T(8,128)S(1)}, f32[1,32,128]{2,1,0:T(8,128)S(1)}, u32[]{:S(2)}, u32[]{:S(2)}) collective-permute-start(f32[1,32,128]{2,1,0:T(8,128)S(1)} %get-tuple-element.57), channel_id=1, source_target_pairs={{0,8},{8,16},{16,24},{1,9},{9,17},{17,25},{2,10},{10,18},{18,26},{... | collective-permute-start | bytes 49160 | tf_op jit(solution)/shard_map/ppermute | solution.py:22
  377.5 5.1 %collective-permute-done.97 = f32[10,34,1]{2,1,0:T(8,128)S(1)} collective-permute-done((f32[10,34,1]{2,1,0:T(8,128)S(1)}, f32[10,34,1]{2,1,0:T(8,128)S(1)}, u32[]{:S(2)}, u32[]{:S(2)}) %collective-permute-start.97) | collective-permute-done | bytes 1392 | tf_op jit(solution)/shard_map/ppermute | solution.py:23
  (284 shorter events, 221.5 us)
Async XLA Ops:
  65.9 10.7 %collective-permute-start.16 = (f32[10,34,1]{2,1,0:T(8,128)S(1)}, f32[10,34,1]{2,1,0:T(8,128)S(1)}, u32[]{:S(2)}, u32[]{:S(2)}) collective-permute-start(f32[10,34,1]{2,1,0:T(8,128)S(1)} %get-tuple-element.48), channel_id=1, source_target_pairs={{1,0},{2,1},{3,2},{5,4},{6,5},{7,6},{9,8},{10,9},{11,10},{13,12},{... | collective-permute-start | bytes 4088 | tf_op jit(solution)/shard_map/ppermute | solution.py:23
  67.2 10.6 %collective-permute-start.17 = (f32[10,34,1]{2,1,0:T(8,128)S(1)}, f32[10,34,1]{2,1,0:T(8,128)S(1)}, u32[]{:S(2)}, u32[]{:S(2)}) collective-permute-start(f32[10,34,1]{2,1,0:T(8,128)S(1)} %get-tuple-element.49), channel_id=1, source_target_pairs={{0,1},{1,2},{2,3},{4,5},{5,6},{6,7},{8,9},{9,10},{10,11},{12,13},{... | collective-permute-start | bytes 4088 | tf_op jit(solution)/shard_map/ppermute | solution.py:22
  90.1 10.7 %collective-permute-start.22 = (f32[10,34,1]{2,1,0:T(8,128)S(1)}, f32[10,34,1]{2,1,0:T(8,128)S(1)}, u32[]{:S(2)}, u32[]{:S(2)}) collective-permute-start(f32[10,34,1]{2,1,0:T(8,128)S(1)} %get-tuple-element.46), channel_id=1, source_target_pairs={{1,0},{2,1},{3,2},{5,4},{6,5},{7,6},{9,8},{10,9},{11,10},{13,12},{... | collective-permute-start | bytes 4088 | tf_op jit(solution)/shard_map/ppermute | solution.py:23
  91.4 10.6 %collective-permute-start.23 = (f32[10,34,1]{2,1,0:T(8,128)S(1)}, f32[10,34,1]{2,1,0:T(8,128)S(1)}, u32[]{:S(2)}, u32[]{:S(2)}) collective-permute-start(f32[10,34,1]{2,1,0:T(8,128)S(1)} %get-tuple-element.47), channel_id=1, source_target_pairs={{0,1},{1,2},{2,3},{4,5},{5,6},{6,7},{8,9},{9,10},{10,11},{12,13},{... | collective-permute-start | bytes 4088 | tf_op jit(solution)/shard_map/ppermute | solution.py:22
  115.8 10.9 %collective-permute-start.28 = (f32[10,34,1]{2,1,0:T(8,128)S(1)}, f32[10,34,1]{2,1,0:T(8,128)S(1)}, u32[]{:S(2)}, u32[]{:S(2)}) collective-permute-start(f32[10,34,1]{2,1,0:T(8,128)S(1)} %get-tuple-element.44), channel_id=1, source_target_pairs={{1,0},{2,1},{3,2},{5,4},{6,5},{7,6},{9,8},{10,9},{11,10},{13,12},{... | collective-permute-start | bytes 4088 | tf_op jit(solution)/shard_map/ppermute | solution.py:23
  117.1 11.2 %collective-permute-start.29 = (f32[10,34,1]{2,1,0:T(8,128)S(1)}, f32[10,34,1]{2,1,0:T(8,128)S(1)}, u32[]{:S(2)}, u32[]{:S(2)}) collective-permute-start(f32[10,34,1]{2,1,0:T(8,128)S(1)} %get-tuple-element.45), channel_id=1, source_target_pairs={{0,1},{1,2},{2,3},{4,5},{5,6},{6,7},{8,9},{9,10},{10,11},{12,13},{... | collective-permute-start | bytes 4088 | tf_op jit(solution)/shard_map/ppermute | solution.py:22
  140.6 10.7 %collective-permute-start.34 = (f32[10,34,1]{2,1,0:T(8,128)S(1)}, f32[10,34,1]{2,1,0:T(8,128)S(1)}, u32[]{:S(2)}, u32[]{:S(2)}) collective-permute-start(f32[10,34,1]{2,1,0:T(8,128)S(1)} %get-tuple-element.42), channel_id=1, source_target_pairs={{1,0},{2,1},{3,2},{5,4},{6,5},{7,6},{9,8},{10,9},{11,10},{13,12},{... | collective-permute-start | bytes 4088 | tf_op jit(solution)/shard_map/ppermute | solution.py:23
  141.9 10.6 %collective-permute-start.35 = (f32[10,34,1]{2,1,0:T(8,128)S(1)}, f32[10,34,1]{2,1,0:T(8,128)S(1)}, u32[]{:S(2)}, u32[]{:S(2)}) collective-permute-start(f32[10,34,1]{2,1,0:T(8,128)S(1)} %get-tuple-element.43), channel_id=1, source_target_pairs={{0,1},{1,2},{2,3},{4,5},{5,6},{6,7},{8,9},{9,10},{10,11},{12,13},{... | collective-permute-start | bytes 4088 | tf_op jit(solution)/shard_map/ppermute | solution.py:22
  164.8 10.7 %collective-permute-start.40 = (f32[10,34,1]{2,1,0:T(8,128)S(1)}, f32[10,34,1]{2,1,0:T(8,128)S(1)}, u32[]{:S(2)}, u32[]{:S(2)}) collective-permute-start(f32[10,34,1]{2,1,0:T(8,128)S(1)} %get-tuple-element.40), channel_id=1, source_target_pairs={{1,0},{2,1},{3,2},{5,4},{6,5},{7,6},{9,8},{10,9},{11,10},{13,12},{... | collective-permute-start | bytes 4088 | tf_op jit(solution)/shard_map/ppermute | solution.py:23
  166.1 10.6 %collective-permute-start.41 = (f32[10,34,1]{2,1,0:T(8,128)S(1)}, f32[10,34,1]{2,1,0:T(8,128)S(1)}, u32[]{:S(2)}, u32[]{:S(2)}) collective-permute-start(f32[10,34,1]{2,1,0:T(8,128)S(1)} %get-tuple-element.41), channel_id=1, source_target_pairs={{0,1},{1,2},{2,3},{4,5},{5,6},{6,7},{8,9},{9,10},{10,11},{12,13},{... | collective-permute-start | bytes 4088 | tf_op jit(solution)/shard_map/ppermute | solution.py:22
  195.5 13.8 %collective-permute-start.53 = (f32[10,34,1]{2,1,0:T(8,128)S(1)}, f32[10,34,1]{2,1,0:T(8,128)S(1)}, u32[]{:S(2)}, u32[]{:S(2)}) collective-permute-start(f32[10,34,1]{2,1,0:T(8,128)S(1)} %get-tuple-element.38), channel_id=1, source_target_pairs={{0,1},{1,2},{2,3},{4,5},{5,6},{6,7},{8,9},{9,10},{10,11},{12,13},{... | collective-permute-start | bytes 4088 | tf_op jit(solution)/shard_map/ppermute | solution.py:22
  200.8 13.6 %collective-permute-start.55 = (f32[10,34,1]{2,1,0:T(8,128)S(1)}, f32[10,34,1]{2,1,0:T(8,128)S(1)}, u32[]{:S(2)}, u32[]{:S(2)}) collective-permute-start(f32[10,34,1]{2,1,0:T(8,128)S(1)} %get-tuple-element.39), channel_id=1, source_target_pairs={{1,0},{2,1},{3,2},{5,4},{6,5},{7,6},{9,8},{10,9},{11,10},{13,12},{... | collective-permute-start | bytes 4088 | tf_op jit(solution)/shard_map/ppermute | solution.py:23
  202.1 16.0 %collective-permute-start.54 = (f32[10,34,1]{2,1,0:T(8,128)S(1)}, f32[10,34,1]{2,1,0:T(8,128)S(1)}, u32[]{:S(2)}, u32[]{:S(2)}) collective-permute-start(f32[10,34,1]{2,1,0:T(8,128)S(1)} %get-tuple-element.36), channel_id=1, source_target_pairs={{1,0},{2,1},{3,2},{5,4},{6,5},{7,6},{9,8},{10,9},{11,10},{13,12},{... | collective-permute-start | bytes 4088 | tf_op jit(solution)/shard_map/ppermute | solution.py:23
  203.4 22.3 %collective-permute-start.47 = (f32[1,32,128]{2,1,0:T(8,128)S(1)}, f32[1,32,128]{2,1,0:T(8,128)S(1)}, u32[]{:S(2)}, u32[]{:S(2)}) collective-permute-start(f32[1,32,128]{2,1,0:T(8,128)S(1)} %get-tuple-element.104), channel_id=1, source_target_pairs={{8,0},{16,8},{24,16},{9,1},{17,9},{25,17},{10,2},{18,10},{26,18},{... | collective-permute-start | bytes 49160 | tf_op jit(solution)/shard_map/ppermute | solution.py:23
  204.7 21.0 %collective-permute-start.45 = (f32[1,32,128]{2,1,0:T(8,128)S(1)}, f32[1,32,128]{2,1,0:T(8,128)S(1)}, u32[]{:S(2)}, u32[]{:S(2)}) collective-permute-start(f32[1,32,128]{2,1,0:T(8,128)S(1)} %get-tuple-element.105), channel_id=1, source_target_pairs={{0,8},{8,16},{16,24},{1,9},{9,17},{17,25},{2,10},{10,18},{18,26},{... | collective-permute-start | bytes 49160 | tf_op jit(solution)/shard_map/ppermute | solution.py:22
  209.3 16.5 %collective-permute-start.44 = (f32[1,32,128]{2,1,0:T(8,128)S(1)}, f32[1,32,128]{2,1,0:T(8,128)S(1)}, u32[]{:S(2)}, u32[]{:S(2)}) collective-permute-start(f32[1,32,128]{2,1,0:T(8,128)S(1)} %get-tuple-element.96), channel_id=1, source_target_pairs={{0,8},{8,16},{16,24},{1,9},{9,17},{17,25},{2,10},{10,18},{18,26},{... | collective-permute-start | bytes 49160 | tf_op jit(solution)/shard_map/ppermute | solution.py:22
  214.4 11.3 %collective-permute-start.46 = (f32[1,32,128]{2,1,0:T(8,128)S(1)}, f32[1,32,128]{2,1,0:T(8,128)S(1)}, u32[]{:S(2)}, u32[]{:S(2)}) collective-permute-start(f32[1,32,128]{2,1,0:T(8,128)S(1)} %get-tuple-element.97), channel_id=1, source_target_pairs={{8,0},{16,8},{24,16},{9,1},{17,9},{25,17},{10,2},{18,10},{26,18},{... | collective-permute-start | bytes 49160 | tf_op jit(solution)/shard_map/ppermute | solution.py:23
  229.1 21.8 %collective-permute-start.57 = (f32[1,32,128]{2,1,0:T(8,128)S(1)}, f32[1,32,128]{2,1,0:T(8,128)S(1)}, u32[]{:S(2)}, u32[]{:S(2)}) collective-permute-start(f32[1,32,128]{2,1,0:T(8,128)S(1)} %get-tuple-element.92), channel_id=1, source_target_pairs={{8,0},{16,8},{24,16},{9,1},{17,9},{25,17},{10,2},{18,10},{26,18},{... | collective-permute-start | bytes 49160 | tf_op jit(solution)/shard_map/ppermute | solution.py:23
  230.4 20.5 %collective-permute-start.56 = (f32[1,32,128]{2,1,0:T(8,128)S(1)}, f32[1,32,128]{2,1,0:T(8,128)S(1)}, u32[]{:S(2)}, u32[]{:S(2)}) collective-permute-start(f32[1,32,128]{2,1,0:T(8,128)S(1)} %get-tuple-element.93), channel_id=1, source_target_pairs={{0,8},{8,16},{16,24},{1,9},{9,17},{17,25},{2,10},{10,18},{18,26},{... | collective-permute-start | bytes 49160 | tf_op jit(solution)/shard_map/ppermute | solution.py:22
  239.5 11.3 %collective-permute-start.61 = (f32[10,34,1]{2,1,0:T(8,128)S(1)}, f32[10,34,1]{2,1,0:T(8,128)S(1)}, u32[]{:S(2)}, u32[]{:S(2)}) collective-permute-start(f32[10,34,1]{2,1,0:T(8,128)S(1)} %get-tuple-element.35), channel_id=1, source_target_pairs={{1,0},{2,1},{3,2},{5,4},{6,5},{7,6},{9,8},{10,9},{11,10},{13,12},{... | collective-permute-start | bytes 4088 | tf_op jit(solution)/shard_map/ppermute | solution.py:23
  254.4 19.3 %collective-permute-start.63 = (f32[1,32,128]{2,1,0:T(8,128)S(1)}, f32[1,32,128]{2,1,0:T(8,128)S(1)}, u32[]{:S(2)}, u32[]{:S(2)}) collective-permute-start(f32[1,32,128]{2,1,0:T(8,128)S(1)} %get-tuple-element.86), channel_id=1, source_target_pairs={{8,0},{16,8},{24,16},{9,1},{17,9},{25,17},{10,2},{18,10},{26,18},{... | collective-permute-start | bytes 49160 | tf_op jit(solution)/shard_map/ppermute | solution.py:23
  255.7 18.0 %collective-permute-start.62 = (f32[1,32,128]{2,1,0:T(8,128)S(1)}, f32[1,32,128]{2,1,0:T(8,128)S(1)}, u32[]{:S(2)}, u32[]{:S(2)}) collective-permute-start(f32[1,32,128]{2,1,0:T(8,128)S(1)} %get-tuple-element.87), channel_id=1, source_target_pairs={{0,8},{8,16},{16,24},{1,9},{9,17},{17,25},{2,10},{10,18},{18,26},{... | collective-permute-start | bytes 49160 | tf_op jit(solution)/shard_map/ppermute | solution.py:22
  277.4 18.1 %collective-permute-start.69 = (f32[1,32,128]{2,1,0:T(8,128)S(1)}, f32[1,32,128]{2,1,0:T(8,128)S(1)}, u32[]{:S(2)}, u32[]{:S(2)}) collective-permute-start(f32[1,32,128]{2,1,0:T(8,128)S(1)} %get-tuple-element.80), channel_id=1, source_target_pairs={{8,0},{16,8},{24,16},{9,1},{17,9},{25,17},{10,2},{18,10},{26,18},{... | collective-permute-start | bytes 49160 | tf_op jit(solution)/shard_map/ppermute | solution.py:23
  278.7 16.8 %collective-permute-start.68 = (f32[1,32,128]{2,1,0:T(8,128)S(1)}, f32[1,32,128]{2,1,0:T(8,128)S(1)}, u32[]{:S(2)}, u32[]{:S(2)}) collective-permute-start(f32[1,32,128]{2,1,0:T(8,128)S(1)} %get-tuple-element.81), channel_id=1, source_target_pairs={{0,8},{8,16},{16,24},{1,9},{9,17},{17,25},{2,10},{10,18},{18,26},{... | collective-permute-start | bytes 49160 | tf_op jit(solution)/shard_map/ppermute | solution.py:22
  299.1 18.1 %collective-permute-start.75 = (f32[1,32,128]{2,1,0:T(8,128)S(1)}, f32[1,32,128]{2,1,0:T(8,128)S(1)}, u32[]{:S(2)}, u32[]{:S(2)}) collective-permute-start(f32[1,32,128]{2,1,0:T(8,128)S(1)} %get-tuple-element.74), channel_id=1, source_target_pairs={{8,0},{16,8},{24,16},{9,1},{17,9},{25,17},{10,2},{18,10},{26,18},{... | collective-permute-start | bytes 49160 | tf_op jit(solution)/shard_map/ppermute | solution.py:23
  300.4 16.8 %collective-permute-start.74 = (f32[1,32,128]{2,1,0:T(8,128)S(1)}, f32[1,32,128]{2,1,0:T(8,128)S(1)}, u32[]{:S(2)}, u32[]{:S(2)}) collective-permute-start(f32[1,32,128]{2,1,0:T(8,128)S(1)} %get-tuple-element.75), channel_id=1, source_target_pairs={{0,8},{8,16},{16,24},{1,9},{9,17},{17,25},{2,10},{10,18},{18,26},{... | collective-permute-start | bytes 49160 | tf_op jit(solution)/shard_map/ppermute | solution.py:22
  320.9 18.3 %collective-permute-start.81 = (f32[1,32,128]{2,1,0:T(8,128)S(1)}, f32[1,32,128]{2,1,0:T(8,128)S(1)}, u32[]{:S(2)}, u32[]{:S(2)}) collective-permute-start(f32[1,32,128]{2,1,0:T(8,128)S(1)} %get-tuple-element.68), channel_id=1, source_target_pairs={{8,0},{16,8},{24,16},{9,1},{17,9},{25,17},{10,2},{18,10},{26,18},{... | collective-permute-start | bytes 49160 | tf_op jit(solution)/shard_map/ppermute | solution.py:23
  322.2 17.0 %collective-permute-start.80 = (f32[1,32,128]{2,1,0:T(8,128)S(1)}, f32[1,32,128]{2,1,0:T(8,128)S(1)}, u32[]{:S(2)}, u32[]{:S(2)}) collective-permute-start(f32[1,32,128]{2,1,0:T(8,128)S(1)} %get-tuple-element.69), channel_id=1, source_target_pairs={{0,8},{8,16},{16,24},{1,9},{9,17},{17,25},{2,10},{10,18},{18,26},{... | collective-permute-start | bytes 49160 | tf_op jit(solution)/shard_map/ppermute | solution.py:22
  342.8 18.1 %collective-permute-start.87 = (f32[1,32,128]{2,1,0:T(8,128)S(1)}, f32[1,32,128]{2,1,0:T(8,128)S(1)}, u32[]{:S(2)}, u32[]{:S(2)}) collective-permute-start(f32[1,32,128]{2,1,0:T(8,128)S(1)} %get-tuple-element.62), channel_id=1, source_target_pairs={{8,0},{16,8},{24,16},{9,1},{17,9},{25,17},{10,2},{18,10},{26,18},{... | collective-permute-start | bytes 49160 | tf_op jit(solution)/shard_map/ppermute | solution.py:23
  344.1 16.8 %collective-permute-start.86 = (f32[1,32,128]{2,1,0:T(8,128)S(1)}, f32[1,32,128]{2,1,0:T(8,128)S(1)}, u32[]{:S(2)}, u32[]{:S(2)}) collective-permute-start(f32[1,32,128]{2,1,0:T(8,128)S(1)} %get-tuple-element.63), channel_id=1, source_target_pairs={{0,8},{8,16},{16,24},{1,9},{9,17},{17,25},{2,10},{10,18},{18,26},{... | collective-permute-start | bytes 49160 | tf_op jit(solution)/shard_map/ppermute | solution.py:22
  364.6 18.1 %collective-permute-start.93 = (f32[1,32,128]{2,1,0:T(8,128)S(1)}, f32[1,32,128]{2,1,0:T(8,128)S(1)}, u32[]{:S(2)}, u32[]{:S(2)}) collective-permute-start(f32[1,32,128]{2,1,0:T(8,128)S(1)} %get-tuple-element.56), channel_id=1, source_target_pairs={{8,0},{16,8},{24,16},{9,1},{17,9},{25,17},{10,2},{18,10},{26,18},{... | collective-permute-start | bytes 49160 | tf_op jit(solution)/shard_map/ppermute | solution.py:23
  365.9 16.8 %collective-permute-start.92 = (f32[1,32,128]{2,1,0:T(8,128)S(1)}, f32[1,32,128]{2,1,0:T(8,128)S(1)}, u32[]{:S(2)}, u32[]{:S(2)}) collective-permute-start(f32[1,32,128]{2,1,0:T(8,128)S(1)} %get-tuple-element.57), channel_id=1, source_target_pairs={{0,8},{8,16},{16,24},{1,9},{9,17},{17,25},{2,10},{10,18},{18,26},{... | collective-permute-start | bytes 49160 | tf_op jit(solution)/shard_map/ppermute | solution.py:22
  (72 other events, 454.3 us)
where the time goes:
time: 386 us; the launch traced here: 384 us
  starting transfers between devices  215 us (56%)
  waiting for transfers between devices  150 us (39%)
  other arithmetic  8.8 us (2%)
  between operations  5.08 us (1%)
  local copies, waits for them, and re-layouts  4.66 us (1%)
    ppermute x48, starting transfers between devices, padded_2(): before = lax.ppermute(last, axis, up)  150 us
    ppermute x48, waiting for transfers between devices, padded_2(): after = lax.ppermute(leading, axis, down)  107 us
    ppermute x48, starting transfers between devices, padded_2(): after = lax.ppermute(leading, axis, down)  62 us
    ppermute x48, waiting for transfers between devices, padded_2(): before = lax.ppermute(last, axis, up)  38.9 us
  transfers between devices with their start and end apart: 98, of which 53 were waited for; matrix products, arithmetic and copies ran while one was open for 1% of the time, Pallas kernels for 0%

commit v1 on v0

v1 whole, which is shorter than its diff:
```python
import functools

import jax
import jax.numpy as jnp
from jax import lax
from jax.experimental import pallas as pl
from jax.experimental.pallas import tpu as pltpu
from jax.sharding import PartitionSpec as P

SWEEPS = 8
JACOBI = 8
THETA = 7.125
DELTA = 6.875
LOG_GAIN = 2.0
WIDE = 2
MESH = pl.DeviceIdType.MESH

OFFSETS = [
    (x, y, z)
    for x in (-1, 0, 1)
    for y in (-1, 0, 1)
    for z in (-1, 0, 1)
    if 1 <= abs(x) + abs(y) + abs(z) <= 2
]
OFFSETS.sort(key=lambda o: (o[2] != 0, abs(o[0]) + abs(o[1]) + abs(o[2]), -abs(o[0])))


def sweep_weights(count):
    ratio_base = THETA / DELTA
    ratio_now = 1.0 / ratio_base
    weights = []
    for index in range(count):
        ratio_next = 1.0 / (2.0 * ratio_base - ratio_now)
        weights.append((ratio_next * ratio_now, 2.0 * ratio_next / DELTA))
        ratio_now = ratio_next
    return weights


class Plan:
    def __init__(self, mesh, cells, flow_rows):
        self.size = (mesh.shape["gx"], mesh.shape["gy"], mesh.shape["gz"])
        self.cells = cells
        self.flow_rows = flow_rows
        self.inset = 3 * cells[0] * self.size[0] // 4
        cx, count = cells[0], self.size[0]
        mean = 3 * cx // 4
        jitter = (mean - 2) // 2
        centre = cx * count // 8
        self.shifts = {}
        for shift in range(1 - count, count):
            low, high = cx, 0
            for tile in range(max(0, -shift), min(count, count - shift)):
                begin = mean * tile + centre - 2 * jitter - cx * (tile + shift)
                end = begin + flow_rows + 2 * jitter
                if max(begin, 0) < min(end, cx):
                    low, high = min(low, max(begin, 0)), max(high, min(end, cx))
            if low < high:
                self.shifts[shift] = (low, high)
        self.shifts[0] = (0, cx)
        self.lowest, self.highest = min(self.shifts), max(self.shifts)
        self.moves = [s for s in sorted(self.shifts, key=abs) if s != 0]
        self.rounds = [(2, 2), (1, 2), (1, 2), (1, 1), (2, 2), (1, 2), (1, 2), (1, 2), (1, 2)]
        self.bases = [sum(n for n, _ in self.rounds[:i]) for i in range(len(self.rounds))]
        self.total = sum(n for n, _ in self.rounds)


def kernel(
    plan,
    cuts_ref, noise_ref, kappa_ref, init_ref, source_ref,
    field_ref, pressure_ref,
    dir_a, dir_b, resid, kap, prs_a, prs_b, coef, charge, perm, maskv,
    send, packed, land_x, land_y, land_xy, land_p,
    move_out, move_in, last, landed,
    send_sem, recv_sem, move_send, move_recv, last_send, last_recv,
):
    cx, cy, cz = plan.cells
    ext_x, ext_y = cx + 2 * WIDE, cy + 8
    me = [lax.axis_index("gx"), lax.axis_index("gy"), lax.axis_index("gz")]
    tiles_y = cy // 8

    def there(offset):
        flag = None
        for at, by, size in zip(me, offset, plan.size):
            if by == 0:
                continue
            one = (at + by < size) if by > 0 else (at + by >= 0)
            flag = one if flag is None else flag & one
        return flag

    def device(offset):
        return tuple(at + by for at, by in zip(me, offset))

    has = {o: there(o) for o in OFFSETS}
    greet = [o for o in OFFSETS] + [(s, 0, 0) for s in plan.moves if abs(s) > 1]
    for s in plan.moves:
        has[(s, 0, 0)] = there((s, 0, 0))
        has[(-s, 0, 0)] = there((-s, 0, 0))

    barrier = pltpu.get_barrier_semaphore()
    expected = jnp.int32(0)
    for o in greet:
        expected = expected + has[o].astype(jnp.int32)

        @pl.when(has[o])
        def _(o=o):
            pl.semaphore_signal(barrier, inc=1, device_id=device(o), device_id_type=MESH)

    pl.semaphore_wait(barrier, expected)

    lane = lax.broadcasted_iota(jnp.int32, (8, cz), 1)
    row8 = lax.broadcasted_iota(jnp.int32, (8, cz), 0)

    def offsets_of(width):
        return [(i, o) for i, o in enumerate(OFFSETS) if sum(map(abs, o)) <= width]

    def copy_of(rnd, index, o):
        n, w = plan.rounds[rnd]
        arrays = pl.ds(plan.bases[rnd], n)
        planes = {0: pl.ds(0, cx), 1: pl.ds(cx - w, w), -1: pl.ds(0, w)}[o[0]]
        rows = {0: pl.ds(0, cy), 1: pl.ds(cy - 8, 8), -1: pl.ds(0, 8)}[o[1]]
        fx, fy = (0 if o[0] > 0 else 1), (0 if o[1] > 0 else 1)
        if o[2] != 0:
            side = 0 if o[2] < 0 else 1
            src = packed.at[side, arrays]
            dst = land_p.at[1 - o[0], 1 - o[1], side, arrays]
        elif o[0] != 0 and o[1] != 0:
            src = send.at[arrays, planes, rows]
            dst = land_xy.at[fx, fy, arrays, pl.ds(0, w)]
        elif o[0] != 0:
            src = send.at[arrays, planes, rows]
            dst = land_x.at[fx, arrays, pl.ds(0, w)]
        else:
            src = send.at[arrays, planes, rows]
            dst = land_y.at[fy, arrays]
        return pltpu.make_async_remote_copy(
            src_ref=src, dst_ref=dst,
            send_sem=send_sem.at[rnd, index], recv_sem=recv_sem.at[rnd, index],
            device_id=device(o), device_id_type=MESH,
        )

    def start(rnd):
        n, w = plan.rounds[rnd]

        def begin(index, o):
            @pl.when(has[o])
            def _():
                copy_of(rnd, index, o).start()

        for index, o in offsets_of(w):
            if o[2] == 0:
                begin(index, o)
        for a in range(n):
            slot = plan.bases[rnd] + a
            low = jnp.zeros((8, cz), jnp.float32)
            high = jnp.zeros((8, cz), jnp.float32)
            for k in range(cx):
                for j in range(tiles_y):
                    by = (j * cx + k) * w
                    value = send[slot, k, 8 * j : 8 * j + 8]
                    low = jnp.where((lane >= by) & (lane < by + w), pltpu.roll(value, by, 1), low)
                    back = (cz - by) % cz
                    high = jnp.where(
                        (lane >= cz - w - by) & (lane < cz - by), pltpu.roll(value, back, 1), high
                    )
            packed[0, slot] = low
            packed[1, slot] = high
        for index, o in offsets_of(w):
            if o[2] != 0:
                begin(index, o)

    def finish(rnd):
        n, w = plan.rounds[rnd]
        for index, o in offsets_of(w):
            back = tuple(-v for v in o)

            @pl.when(has[back])
            def _(index=index, o=o):
                copy_of(rnd, index, o).wait_recv()

        for index, o in offsets_of(w):
            @pl.when(has[o])
            def _(index=index, o=o):
                copy_of(rnd, index, o).wait_send()

    def assemble(rnd, a, put, fill=0.0):
        n, w = plan.rounds[rnd]
        slot = plan.bases[rnd] + a
        blank = jnp.full((8, cz), fill, jnp.float32)
        arrived = {}
        for o in OFFSETS:
            if o[2] != 0 and sum(map(abs, o)) <= w:
                side = 0 if o[2] > 0 else 1
                arrived[o] = jnp.where(has[o], land_p[1 + o[0], 1 + o[1], side, slot], blank)

        def unpack(dx, dy, k, j):
            by = (j * cx + k) * w
            value = blank
            if (dx, dy, 1) in arrived:
                right = pltpu.roll(arrived[dx, dy, 1], (cz - by) % cz, 1)
                value = jnp.where(lane < w, right, value)
                left = pltpu.roll(arrived[dx, dy, -1], by, 1)
                value = jnp.where(lane >= cz - w, left, value)
            return value

        def between(after, before):
            return jnp.where(row8 < w, after, jnp.where(row8 >= 8 - w, before, blank))

        def columns(dx, k, plane):
            for j in range(tiles_y):
                put(1, plane, 8 * j, unpack(dx, 0, k, j))
            put(1, plane, cy, between(unpack(dx, 1, k, 0), unpack(dx, -1, k, tiles_y - 1)))

        for k in range(cx):
            after = jnp.where(has[0, 1, 0], land_y[1, slot, k], blank)
            before = jnp.where(has[0, -1, 0], land_y[0, slot, k], blank)
            put(0, WIDE + k, cy, between(after, before))
            columns(0, k, WIDE + k)
        for dx in (-1, 1):
            fx = 0 if dx < 0 else 1
            for q in range(w):
                plane = WIDE - w + q if dx < 0 else WIDE + cx + q
                k = cx - w + q if dx < 0 else q
                big = jnp.where(has[dx, 0, 0], land_x[fx, slot, q], jnp.full((cy, cz), fill, jnp.float32))
                for j in range(tiles_y):
                    put(0, plane, 8 * j, big[8 * j : 8 * j + 8])
                if w > 1:
                    after = jnp.where(has[dx, 1, 0], land_xy[fx, 1, slot, q], blank)
                    before = jnp.where(has[dx, -1, 0], land_xy[fx, 0, slot, q], blank)
                    put(0, plane, cy, between(after, before))
                    columns(dx, k, plane)
                else:
                    put(0, plane, cy, blank)
                    for j in range(tiles_y + 1):
                        put(1, plane, 8 * j, blank)

    send[0] = noise_ref[...]
    send[1] = kappa_ref[...]
    start(0)

    inset_begin = cuts_ref[0]
    cut_here = cuts_ref[me[0] + 1]
    count_here = cuts_ref[me[0] + 2] - cut_here

    def pick(ref, shift, r):
        row = cx * (me[0] + shift) + r - inset_begin - cut_here
        value = ref[jnp.clip(row, 0, plan.flow_rows - 1)]
        return jnp.where((row >= 0) & (row < count_here), value, 0.0)

    def move_of(index, shift):
        low, high = plan.shifts[shift]
        return pltpu.make_async_remote_copy(
            src_ref=move_out.at[index, :, pl.ds(low, high - low)],
            dst_ref=move_in.at[index, :, pl.ds(low, high - low)],
            send_sem=move_send.at[index], recv_sem=move_recv.at[index],
            device_id=device((shift, 0, 0)), device_id_type=MESH,
        )

    for index, shift in enumerate(plan.moves):
        low, high = plan.shifts[shift]
        for a, ref in enumerate((init_ref, source_ref)):
            @pl.loop(low, high)
            def _(r, a=a, ref=ref, index=index, shift=shift):
                move_out[index, a, r] = pick(ref, shift, r)

        @pl.when(has[shift, 0, 0])
        def _(index=index, shift=shift):
            move_of(index, shift).start()

    slot_q = plan.bases[4]
    for a, ref in enumerate((init_ref, source_ref)):
        @pl.loop(0, cx)
        def _(r, a=a, ref=ref):
            send[slot_q + a, r] = pick(ref, 0, r)

    row = lax.broadcasted_iota(jnp.int32, (ext_y, cz), 0)
    col = lax.broadcasted_iota(jnp.int32, (ext_y, cz), 1)
    in_rows = (row < cy) | ((row < cy + WIDE) & has[0, 1, 0]) | ((row >= ext_y - WIDE) & has[0, -1, 0])
    in_cols = ((col < WIDE) & has[0, 0, 1]) | ((col >= cz - WIDE) & has[0, 0, -1])
    maskv[0] = jnp.where(in_rows, 1.0, 0.0)
    maskv[1] = jnp.where(in_rows & in_cols, 1.0, 0.0)

    for k in range(cx):
        value = noise_ref[k]
        resid[0, WIDE + k, 0:cy] = value
        dir_a[0, WIDE + k, 0:cy] = value * (1.0 / THETA)
        field_ref[k] = value * (1.0 / THETA)
        kap[0, WIDE + k, 0:cy] = kappa_ref[k] + 6.0

    first_col, last_col = col == 0, col == cz - 1

    def sides(ref, e):
        core, outer = ref[0, e], ref[1, e]
        core_r, outer_r = pltpu.roll(core, cz - 1, 1), pltpu.roll(outer, cz - 1, 1)
        core_l, outer_l = pltpu.roll(core, 1, 1), pltpu.roll(outer, 1, 1)
        return (
            (core, pltpu.roll(core, 1, 0), pltpu.roll(core, ext_y - 1, 0),
             jnp.where(first_col, outer_l, core_l), jnp.where(last_col, outer_r, core_r)),
            (outer, pltpu.roll(outer, 1, 0), pltpu.roll(outer, ext_y - 1, 0),
             jnp.where(first_col, core_l, outer_l), jnp.where(last_col, core_r, outer_r)),
        )

    weights = sweep_weights(SWEEPS)

    def inside(e):
        at = me[0] * cx - WIDE + e
        return (at >= 0) & (at < plan.size[0] * cx)

    def cheb_wide(old, new, weight):
        @pl.loop(1, ext_x - 1)
        def _(e):
            okay = jnp.where(inside(e), 1.0, 0.0)
            for zt, (mid, up, down, left, right) in enumerate(sides(old, e)):
                beside = old[zt, e - 1] + old[zt, e + 1] + (up + down) + (left + right)
                change = (kap[zt, e] * mid - beside) * (maskv[zt] * okay)
                rest = resid[zt, e] - change
                resid[zt, e] = rest
                new[zt, e] = weight[0] * mid + weight[1] * rest

        @pl.loop(0, cx)
        def _(k):
            field_ref[k] = field_ref[k] + new[0, k + WIDE, 0:cy]

    def cheb_core(old, new, weight, slot):
        @pl.loop(0, cx)
        def _(k):
            e = k + WIDE
            mid, up, down, left, right = sides(old, e)[0]
            beside = old[0, e - 1] + old[0, e + 1] + (up + down) + (left + right)
            rest = (resid[0, e] - (kap[0, e] * mid - beside))[0:cy]
            resid[0, e, 0:cy] = rest
            value = weight[0] * mid[0:cy] + weight[1] * rest
            total = field_ref[k] + value
            field_ref[k] = total
            if slot is None:
                raised = jnp.exp(LOG_GAIN * total)
                send[plan.bases[5], k] = raised
                perm[0, e, 0:cy] = raised
            else:
                new[0, e, 0:cy] = value
                send[slot, k] = value

    finish(0)

    def put_noise(zt, e, r, value):
        resid[zt, e, r : r + 8] = value
        dir_a[zt, e, r : r + 8] = value * (1.0 / THETA)

    def put_kappa(zt, e, r, value):
        kap[zt, e, r : r + 8] = value + 6.0

    assemble(0, 0, put_noise)
    assemble(0, 1, put_kappa)
    cheb_wide(dir_a, dir_b, weights[0])
    cheb_core(dir_b, dir_a, weights[1], plan.bases[1])
    start(1)
    for rnd in (1, 2):
        before = weights[2 * rnd - 1]

        def put_dir(zt, e, r, value, before=before):
            dir_a[zt, e, r : r + 8] = value
            if 1 <= e < ext_x - 1:
                resid[zt, e, r : r + 8] = (value - before[0] * dir_b[zt, e, r : r + 8]) * (1.0 / before[1])

        if rnd == 2:
            for index, shift in enumerate(plan.moves):
                low, high = plan.shifts[shift]

                @pl.when(has[-shift, 0, 0])
                def _(index=index, shift=shift, low=low, high=high):
                    move_of(index, shift).wait_recv()
                    for a in range(2):
                        send[slot_q + a, low:high] = send[slot_q + a, low:high] + move_in[index, a, low:high]

                @pl.when(has[shift, 0, 0])
                def _(index=index, shift=shift):
                    move_of(index, shift).wait_send()

            start(4)
        finish(rnd)
        assemble(rnd, 0, put_dir)
        cheb_wide(dir_a, dir_b, weights[2 * rnd])
        cheb_core(dir_b, dir_a, weights[2 * rnd + 1], plan.bases[rnd + 1])
        start(rnd + 1)

    def put_last(zt, e, r, value):
        dir_a[zt, e, r : r + 8] = value

    finish(3)
    assemble(3, 0, put_last)
    cheb_core(dir_a, None, weights[6], None)
    start(5)

    finish(4)

    def put_init(zt, e, r, value):
        prs_a[zt, e, r : r + 8] = value

    def put_charge(zt, e, r, value):
        charge[zt, e, r : r + 8] = value

    assemble(4, 0, put_init)
    assemble(4, 1, put_charge)
    for k in range(cx):
        prs_a[0, WIDE + k, 0:cy] = send[slot_q, k]
        charge[0, WIDE + k, 0:cy] = send[slot_q + 1, k]

    finish(5)

    def put_perm(zt, e, r, value):
        perm[zt, e, r : r + 8] = value

    assemble(5, 0, put_perm, fill=1.0)

    top = (row == 0) & (me[1] == 0)
    bottom = (row == cy - 1) & (me[1] == plan.size[1] - 1)
    near = first_col & (me[2] == 0)
    far = last_col & (me[2] == plan.size[2] - 1)

    def harmonic(own, other):
        return 2.0 * own * other / (own + other)

    @pl.loop(1, ext_x - 1)
    def _(e):
        plane = me[0] * cx - WIDE + e - inset_begin
        okay = (plane >= 0) & (plane < plan.inset)
        for zt, (mid, up, down, left, right) in enumerate(sides(perm, e)):
            below = jnp.where(plane == 0, mid, perm[zt, e - 1])
            above = jnp.where(plane == plan.inset - 1, mid, perm[zt, e + 1])
            up = jnp.where(top, mid, up)
            down = jnp.where(bottom, mid, down)
            if zt == 0:
                left = jnp.where(near, mid, left)
                right = jnp.where(far, mid, right)
            parts = [harmonic(mid, v) for v in (below, above, up, down, left, right)]
            total = parts[0] + parts[1] + parts[2] + parts[3] + parts[4] + parts[5]
            valid = (maskv[zt] > 0.5) & okay
            for f in range(6):
                coef[f, zt, e] = jnp.where(valid, parts[f] / total, 0.0)
            charge[zt, e] = jnp.where(valid, charge[zt, e] / total, 0.0)

    def flux(old, zt, e, around):
        _, up, down, left, right = around
        value = charge[zt, e] + coef[0, zt, e] * old[zt, e - 1] + coef[1, zt, e] * old[zt, e + 1]
        value = value + coef[2, zt, e] * up + coef[3, zt, e] * down
        return value + coef[4, zt, e] * left + coef[5, zt, e] * right

    def jacobi_wide(old, new):
        @pl.loop(1, ext_x - 1)
        def _(e):
            for zt, around in enumerate(sides(old, e)):
                new[zt, e] = flux(old, zt, e, around)

    def jacobi_core(old, new, slot):
        @pl.loop(0, cx)
        def _(k):
            e = k + WIDE
            value = flux(old, 0, e, sides(old, e)[0])[0:cy]
            if slot is None:
                last[k] = value
            else:
                new[0, e, 0:cy] = value
                send[slot, k] = value

    for block in range(JACOBI // 2):
        if block > 0:
            finish(5 + block)
            assemble(5 + block, 0, put_init)
        jacobi_wide(prs_a, prs_b)
        final = block == JACOBI // 2 - 1
        jacobi_core(prs_b, prs_a, None if final else plan.bases[6 + block])
        if not final:
            start(6 + block)

    def last_of(index, shift):
        low, high = plan.shifts[shift]
        at = (shift - plan.lowest) * cx + low
        return pltpu.make_async_remote_copy(
            src_ref=last.at[pl.ds(low, high - low)],
            dst_ref=landed.at[pl.ds(at, high - low)],
            send_sem=last_send.at[index], recv_sem=last_recv.at[index],
            device_id=device((-shift, 0, 0)), device_id_type=MESH,
        )

    for index, shift in enumerate(plan.moves):
        @pl.when(has[-shift, 0, 0])
        def _(index=index, shift=shift):
            last_of(index, shift).start()

    landed[-plan.lowest * cx : (1 - plan.lowest) * cx] = last[...]
    for index, shift in enumerate(plan.moves):
        @pl.when(has[shift, 0, 0])
        def _(index=index, shift=shift):
            last_of(index, shift).wait_recv()

    window = (plan.highest - plan.lowest + 1) * cx

    @pl.loop(0, plan.flow_rows)
    def _(j):
        at = inset_begin + cut_here + j - cx * (me[0] + plan.lowest)
        value = landed[jnp.clip(at, 0, window - 1)]
        pressure_ref[j] = jnp.where(j < count_here, value, 0.0)

    for index, shift in enumerate(plan.moves):
        @pl.when(has[-shift, 0, 0])
        def _(index=index, shift=shift):
            last_of(index, shift).wait_send()


def local(mesh, noise, kappa_sq, cuts, pressure_init, source):
    cells, flow_rows = noise.shape, pressure_init.shape[0]
    plan = Plan(mesh, cells, flow_rows)
    cx, cy, cz = cells
    block = (2, cx + 2 * WIDE, cy + 8, cz)
    moves = max(1, len(plan.moves))
    f32 = jnp.float32
    vmem = lambda *shape: pltpu.VMEM(shape, f32)
    sems = lambda *shape: pltpu.SemaphoreType.DMA(shape)
    total = plan.total
    return pl.pallas_call(
        functools.partial(kernel, plan),
        out_shape=(
            jax.ShapeDtypeStruct(noise.shape, f32),
            jax.ShapeDtypeStruct(pressure_init.shape, f32),
        ),
        in_specs=[pl.BlockSpec(memory_space=pltpu.SMEM)] + [pl.BlockSpec(memory_space=pltpu.VMEM)] * 4,
        out_specs=(pl.BlockSpec(memory_space=pltpu.VMEM),) * 2,
        scratch_shapes=[
            vmem(*block), vmem(*block), vmem(*block), vmem(*block), vmem(*block), vmem(*block),
            vmem(6, *block), vmem(*block), vmem(*block), vmem(2, cy + 8, cz),
            vmem(total, cx, cy, cz), vmem(2, total, 8, cz),
            vmem(2, total, WIDE, cy, cz), vmem(2, total, cx, 8, cz),
            vmem(2, 2, total, WIDE, 8, cz), vmem(3, 3, 2, total, 8, cz),
            vmem(moves, 2, cx, cy, cz), vmem(moves, 2, cx, cy, cz),
            vmem(cx, cy, cz), vmem((plan.highest - plan.lowest + 1) * cx, cy, cz),
            sems(len(plan.rounds), len(OFFSETS)), sems(len(plan.rounds), len(OFFSETS)),
            sems(moves), sems(moves), sems(moves), sems(moves),
        ],
        compiler_params=pltpu.CompilerParams(
            collective_id=0, has_side_effects=True, vmem_limit_bytes=48 * 1024 * 1024
        ),
        cost_estimate=pl.CostEstimate(flops=30_000_000, bytes_accessed=1_000_000, transcendentals=32768),
        name="sweeps",
    )(cuts, noise, kappa_sq, pressure_init, source)


def solution(mesh):
    part = P("gx", "gy", "gz")
    return jax.shard_map(
        functools.partial(local, mesh),
        mesh=mesh,
        in_specs=(part, part, P(), part, part),
        out_specs=(part, part),
        check_vma=False,
    )
```

time: 386 us -> 67.8 us (0.18)
  starting transfers between devices: 215 us -> 0 us
  waiting for transfers between devices: 150 us -> 0 us
  Pallas kernels: 0 us -> 61.3 us
  other arithmetic: 8.8 us -> 0 us
  between operations: 5.08 us -> 0.65 us
    ppermute x98 -> x0, starting transfers between devices: 215 us -> none  [the longest x48 150 us: padded_2(): before = lax.ppermute(last, axis, up)]
    ppermute x98 -> x0, waiting for transfers between devices: 150 us -> none  [the longest x48 107 us: padded_2(): after = lax.ppermute(leading, axis, down)]
    pallas_call x0 -> x1, Pallas kernels: none -> 61.3 us  [local(): pl.pallas_call(functools.partial(kernel, plan), out_shape=(jax.ShapeDtype...]
    unnamed x12, local copies, waits for them, and re-layouts: 0.04 us -> 5.61 us
    select_n x12 -> x0, other arithmetic: 4.67 us -> none  [the longest x8 4.17 us: local(): pressure = jnp.where(live_cells, flux / total, 0.0)]
  transfers between devices with their start and end apart: 98 -> 0, of which waited for: 53 -> 0; matrix products, arithmetic and copies ran while one was open for 1% -> 0% of each run, Pallas kernels for 0% -> 0%
where the time goes in v1:
time: 67.8 us; the launch traced here: 67.5 us
  Pallas kernels  61.3 us (90%)
  local copies, waits for them, and re-layouts  5.61 us (8%)
    pallas_call x1, Pallas kernels, local(): pl.pallas_call(functools.partial(kernel, plan), out_shape=(jax.ShapeDtype...  61.3 us
    unnamed x12, local copies, waits for them, and re-layouts  5.61 us

profile of v1, /device:TPU:0, one launch (start us, length us, event | category | flops | bytes accessed | tf_op | source)
XLA Modules:
  0.0 67.5 jit_solution(603946793171824207)
XLA Ops:
  0.6 0.0 copy-start
  0.6 0.9 %copy-done = f32[10,32,128]{2,1,0:T(8,128)S(1)} copy-done((f32[10,32,128]{2,1,0:T(8,128)S(1)}, f32[10,32,128]{2,1,0:T(8,128)}, u32[]{:S(2)}) %copy-start) | copy-done | bytes 163864
  1.5 0.0 copy-start.1
  1.6 0.9 %copy-done.1 = f32[10,32,128]{2,1,0:T(8,128)S(1)} copy-done((f32[10,32,128]{2,1,0:T(8,128)S(1)}, f32[10,32,128]{2,1,0:T(8,128)}, u32[]{:S(2)}) %copy-start.1) | copy-done | bytes 163864
  2.5 0.0 copy-start.2
  2.5 0.9 %copy-done.2 = f32[8,32,128]{2,1,0:T(8,128)S(1)} copy-done((f32[8,32,128]{2,1,0:T(8,128)S(1)}, f32[8,32,128]{2,1,0:T(8,128)}, u32[]{:S(2)}) %copy-start.2) | copy-done | bytes 131096
  3.4 0.0 copy-start.3
  3.4 0.9 %copy-done.3 = f32[8,32,128]{2,1,0:T(8,128)S(1)} copy-done((f32[8,32,128]{2,1,0:T(8,128)S(1)}, f32[8,32,128]{2,1,0:T(8,128)}, u32[]{:S(2)}) %copy-start.3) | copy-done | bytes 131096
  4.3 0.0 copy-start.4
  4.3 0.7 copy-done.4
  4.9 61.3 %sweeps.1 = (f32[8,32,128]{2,1,0:T(8,128)S(1)}, f32[10,32,128]{2,1,0:T(8,128)S(1)}) custom-call(s32[6]{0:T(128)S(1)} %copy-done.4, f32[8,32,128]{2,1,0:T(8,128)S(1)} %copy-done.2, f32[8,32,128]{2,1,0:T(8,128)S(1)} %copy-done.3, f32[10,32,128]{2,1,0:T(8,128)S(1)} %copy-done, f32[10,32,128]{2,1,0:T(8,128)S(1)} %copy-done.1), custom_call_target="tpu_custom_call" | custom-call | flops 30000000 | bytes 1000000 | tf_op jit(solution)/shard_map/sweeps/pallas_call | solution.py:519
  66.2 0.7 copy.9
  66.9 0.7 copy.10
Async XLA Ops:
  0.6 0.9 %copy-start = (f32[10,32,128]{2,1,0:T(8,128)S(1)}, f32[10,32,128]{2,1,0:T(8,128)}, u32[]{:S(2)}) copy-start(f32[10,32,128]{2,1,0:T(8,128)} %init_ref.1) | copy-start | bytes 491524
  1.5 0.9 %copy-start.1 = (f32[10,32,128]{2,1,0:T(8,128)S(1)}, f32[10,32,128]{2,1,0:T(8,128)}, u32[]{:S(2)}) copy-start(f32[10,32,128]{2,1,0:T(8,128)} %source_ref.1) | copy-start | bytes 491524
  2.5 0.9 %copy-start.2 = (f32[8,32,128]{2,1,0:T(8,128)S(1)}, f32[8,32,128]{2,1,0:T(8,128)}, u32[]{:S(2)}) copy-start(f32[8,32,128]{2,1,0:T(8,128)} %noise_ref.1) | copy-start | bytes 393220
  3.4 0.9 %copy-start.3 = (f32[8,32,128]{2,1,0:T(8,128)S(1)}, f32[8,32,128]{2,1,0:T(8,128)}, u32[]{:S(2)}) copy-start(f32[8,32,128]{2,1,0:T(8,128)} %kappa_ref.1) | copy-start | bytes 393220
  4.3 0.7 copy-start.4

commit v2 on v1

--- a/solution.py
+++ b/solution.py
@@ -12,7 +12,7 @@
 THETA = 7.125
 DELTA = 6.875
 LOG_GAIN = 2.0
-WIDE = 2
+WIDE = 4
 MESH = pl.DeviceIdType.MESH
 
 OFFSETS = [
@@ -20,7 +20,7 @@
     for x in (-1, 0, 1)
     for y in (-1, 0, 1)
     for z in (-1, 0, 1)
-    if 1 <= abs(x) + abs(y) + abs(z) <= 2
+    if abs(x) + abs(y) + abs(z) >= 1
 ]
 OFFSETS.sort(key=lambda o: (o[2] != 0, abs(o[0]) + abs(o[1]) + abs(o[2]), -abs(o[0])))
 
@@ -59,16 +59,17 @@
         self.shifts[0] = (0, cx)
         self.lowest, self.highest = min(self.shifts), max(self.shifts)
         self.moves = [s for s in sorted(self.shifts, key=abs) if s != 0]
-        self.rounds = [(2, 2), (1, 2), (1, 2), (1, 1), (2, 2), (1, 2), (1, 2), (1, 2), (1, 2)]
+        self.rounds = [(2, 4), (2, 3), (2, 4), (1, 4), (1, 4)]
         self.bases = [sum(n for n, _ in self.rounds[:i]) for i in range(len(self.rounds))]
         self.total = sum(n for n, _ in self.rounds)
 
 
 def kernel(
     plan,
-    cuts_ref, noise_ref, kappa_ref, init_ref, source_ref,
+    cuts_hbm, noise_hbm, kappa_hbm, init_hbm, source_hbm,
     field_ref, pressure_ref,
     dir_a, dir_b, resid, kap, prs_a, prs_b, coef, charge, perm, maskv,
+    init_in, source_in, cuts_in, load_sem,
     send, packed, land_x, land_y, land_xy, land_p,
     move_out, move_in, last, landed,
     send_sem, recv_sem, move_send, move_recv, last_send, last_recv,
@@ -95,6 +96,17 @@
     for s in plan.moves:
         has[(s, 0, 0)] = there((s, 0, 0))
         has[(-s, 0, 0)] = there((-s, 0, 0))
+
+    init_ref, source_ref, cuts_ref = init_in, source_in, cuts_in
+    loads = [
+        pltpu.make_async_copy(noise_hbm, send.at[0], load_sem.at[0]),
+        pltpu.make_async_copy(kappa_hbm, send.at[1], load_sem.at[1]),
+        pltpu.make_async_copy(init_hbm, init_in, load_sem.at[2]),
+        pltpu.make_async_copy(source_hbm, source_in, load_sem.at[3]),
+        pltpu.make_async_copy(cuts_hbm, cuts_in, load_sem.at[4]),
+    ]
+    for load in loads:
+        load.start()
 
     barrier = pltpu.get_barrier_semaphore()
     expected = jnp.int32(0)
@@ -233,9 +245,11 @@
                     for j in range(tiles_y + 1):
                         put(1, plane, 8 * j, blank)
 
-    send[0] = noise_ref[...]
-    send[1] = kappa_ref[...]
+    loads[0].wait()
+    loads[1].wait()
     start(0)
+    for load in loads[2:]:
+        load.wait()
 
     inset_begin = cuts_ref[0]
     cut_here = cuts_ref[me[0] + 1]
@@ -266,7 +280,7 @@
         def _(index=index, shift=shift):
             move_of(index, shift).start()
 
-    slot_q = plan.bases[4]
+    slot_q = plan.bases[2]
     for a, ref in enumerate((init_ref, source_ref)):
         @pl.loop(0, cx)
         def _(r, a=a, ref=ref):
@@ -280,11 +294,11 @@
     maskv[1] = jnp.where(in_rows & in_cols, 1.0, 0.0)
 
     for k in range(cx):
-        value = noise_ref[k]
+        value = send[0, k]
         resid[0, WIDE + k, 0:cy] = value
         dir_a[0, WIDE + k, 0:cy] = value * (1.0 / THETA)
         field_ref[k] = value * (1.0 / THETA)
-        kap[0, WIDE + k, 0:cy] = kappa_ref[k] + 6.0
+        kap[0, WIDE + k, 0:cy] = send[1, k] + 6.0
 
     first_col, last_col = col == 0, col == cz - 1
 
@@ -305,39 +319,45 @@
         at = me[0] * cx - WIDE + e
         return (at >= 0) & (at < plan.size[0] * cx)
 
-    def cheb_wide(old, new, weight):
-        @pl.loop(1, ext_x - 1)
-        def _(e):
-            okay = jnp.where(inside(e), 1.0, 0.0)
-            for zt, (mid, up, down, left, right) in enumerate(sides(old, e)):
-                beside = old[zt, e - 1] + old[zt, e + 1] + (up + down) + (left + right)
-                change = (kap[zt, e] * mid - beside) * (maskv[zt] * okay)
-                rest = resid[zt, e] - change
-                resid[zt, e] = rest
-                new[zt, e] = weight[0] * mid + weight[1] * rest
-
-        @pl.loop(0, cx)
-        def _(k):
-            field_ref[k] = field_ref[k] + new[0, k + WIDE, 0:cy]
+    def planes_of(low, high):
+        for first, end, own in ((low, WIDE, False), (WIDE, WIDE + cx, True), (WIDE + cx, high, False)):
+            if first < end:
+                yield first, end, own
+
+    def cheb_wide(old, new, weight, low, high):
+        for first, end, own in planes_of(low, high):
+            @pl.loop(first, end, unroll=True)
+            def _(e, own=own):
+                okay = jnp.where(inside(e), 1.0, 0.0)
+                for zt, (mid, up, down, left, right) in enumerate(sides(old, e)):
+                    beside = old[zt, e - 1] + old[zt, e + 1] + (up + down) + (left + right)
+                    part = maskv[zt] if own else maskv[zt] * okay
+                    rest = resid[zt, e] - (kap[zt, e] * mid - beside) * part
+                    resid[zt, e] = rest
+                    value = weight[0] * mid + weight[1] * rest
+                    new[zt, e] = value
+                    if own and zt == 0:
+                        field_ref[e - WIDE] = field_ref[e - WIDE] + value[0:cy]
 
     def cheb_core(old, new, weight, slot):
-        @pl.loop(0, cx)
+        @pl.loop(0, cx, unroll=True)
         def _(k):
             e = k + WIDE
             mid, up, down, left, right = sides(old, e)[0]
             beside = old[0, e - 1] + old[0, e + 1] + (up + down) + (left + right)
             rest = (resid[0, e] - (kap[0, e] * mid - beside))[0:cy]
-            resid[0, e, 0:cy] = rest
             value = weight[0] * mid[0:cy] + weight[1] * rest
             total = field_ref[k] + value
             field_ref[k] = total
             if slot is None:
                 raised = jnp.exp(LOG_GAIN * total)
-                send[plan.bases[5], k] = raised
+                send[plan.bases[3], k] = raised
                 perm[0, e, 0:cy] = raised
             else:
+                resid[0, e, 0:cy] = rest
                 new[0, e, 0:cy] = value
                 send[slot, k] = value
+                send[slot + 1, k] = rest
 
     finish(0)
 
@@ -350,47 +370,42 @@
 
     assemble(0, 0, put_noise)
     assemble(0, 1, put_kappa)
-    cheb_wide(dir_a, dir_b, weights[0])
-    cheb_core(dir_b, dir_a, weights[1], plan.bases[1])
+    for sweep in range(3):
+        old, new = (dir_a, dir_b) if sweep % 2 == 0 else (dir_b, dir_a)
+        cheb_wide(old, new, weights[sweep], sweep + 1, ext_x - sweep - 1)
+    cheb_core(dir_b, dir_a, weights[3], plan.bases[1])
     start(1)
-    for rnd in (1, 2):
-        before = weights[2 * rnd - 1]
-
-        def put_dir(zt, e, r, value, before=before):
-            dir_a[zt, e, r : r + 8] = value
-            if 1 <= e < ext_x - 1:
-                resid[zt, e, r : r + 8] = (value - before[0] * dir_b[zt, e, r : r + 8]) * (1.0 / before[1])
-
-        if rnd == 2:
-            for index, shift in enumerate(plan.moves):
-                low, high = plan.shifts[shift]
-
-                @pl.when(has[-shift, 0, 0])
-                def _(index=index, shift=shift, low=low, high=high):
-                    move_of(index, shift).wait_recv()
-                    for a in range(2):
-                        send[slot_q + a, low:high] = send[slot_q + a, low:high] + move_in[index, a, low:high]
-
-                @pl.when(has[shift, 0, 0])
-                def _(index=index, shift=shift):
-                    move_of(index, shift).wait_send()
-
-            start(4)
-        finish(rnd)
-        assemble(rnd, 0, put_dir)
-        cheb_wide(dir_a, dir_b, weights[2 * rnd])
-        cheb_core(dir_b, dir_a, weights[2 * rnd + 1], plan.bases[rnd + 1])
-        start(rnd + 1)
-
-    def put_last(zt, e, r, value):
+
+    for index, shift in enumerate(plan.moves):
+        low, high = plan.shifts[shift]
+
+        @pl.when(has[-shift, 0, 0])
+        def _(index=index, shift=shift, low=low, high=high):
+            move_of(index, shift).wait_recv()
+            for a in range(2):
+                send[slot_q + a, low:high] = send[slot_q + a, low:high] + move_in[index, a, low:high]
+
+        @pl.when(has[shift, 0, 0])
+        def _(index=index, shift=shift):
+            move_of(index, shift).wait_send()
+
+    start(2)
+
+    def put_dir(zt, e, r, value):
         dir_a[zt, e, r : r + 8] = value
 
-    finish(3)
-    assemble(3, 0, put_last)
+    def put_resid(zt, e, r, value):
+        resid[zt, e, r : r + 8] = value
+
+    finish(1)
+    assemble(1, 0, put_dir)
+    assemble(1, 1, put_resid)
+    cheb_wide(dir_a, dir_b, weights[4], 2, ext_x - 2)
+    cheb_wide(dir_b, dir_a, weights[5], 3, ext_x - 3)
     cheb_core(dir_a, None, weights[6], None)
-    start(5)
-
-    finish(4)
+    start(3)
+
+    finish(2)
 
     def put_init(zt, e, r, value):
         prs_a[zt, e, r : r + 8] = value
@@ -398,18 +413,18 @@
     def put_charge(zt, e, r, value):
         charge[zt, e, r : r + 8] = value
 
-    assemble(4, 0, put_init)
-    assemble(4, 1, put_charge)
+    assemble(2, 0, put_init)
+    assemble(2, 1, put_charge)
     for k in range(cx):
         prs_a[0, WIDE + k, 0:cy] = send[slot_q, k]
         charge[0, WIDE + k, 0:cy] = send[slot_q + 1, k]
 
-    finish(5)
+    finish(3)
 
     def put_perm(zt, e, r, value):
         perm[zt, e, r : r + 8] = value
 
-    assemble(5, 0, put_perm, fill=1.0)
+    assemble(3, 0, put_perm, fill=1.0)
 
     top = (row == 0) & (me[1] == 0)
     bottom = (row == cy - 1) & (me[1] == plan.size[1] - 1)
@@ -419,57 +434,84 @@
     def harmonic(own, other):
         return 2.0 * own * other / (own + other)
 
-    @pl.loop(1, ext_x - 1)
+    @pl.loop(0, ext_x - 1, unroll=True)
+    def _(e):
+        plane = me[0] * cx - WIDE + e - inset_begin
+        pair = (plane >= 0) & (plane < plan.inset - 1)
+        for zt in range(2):
+            coef[0, zt, e] = jnp.where(pair, harmonic(perm[zt, e], perm[zt, e + 1]), 0.0)
+
+    @pl.loop(1, ext_x - 1, unroll=True)
     def _(e):
         plane = me[0] * cx - WIDE + e - inset_begin
         okay = (plane >= 0) & (plane < plan.inset)
-        for zt, (mid, up, down, left, right) in enumerate(sides(perm, e)):
-            below = jnp.where(plane == 0, mid, perm[zt, e - 1])
-            above = jnp.where(plane == plan.inset - 1, mid, perm[zt, e + 1])
-            up = jnp.where(top, mid, up)
-            down = jnp.where(bottom, mid, down)
-            if zt == 0:
-                left = jnp.where(near, mid, left)
-                right = jnp.where(far, mid, right)
-            parts = [harmonic(mid, v) for v in (below, above, up, down, left, right)]
-            total = parts[0] + parts[1] + parts[2] + parts[3] + parts[4] + parts[5]
+        (core, _, core_down, _, core_right), (outer, _, outer_down, _, outer_right) = sides(perm, e)
+        core_z = jnp.where(okay, harmonic(core, core_right), 0.0)
+        outer_z = jnp.where(okay, harmonic(outer, outer_right), 0.0)
+        core_back, outer_back = pltpu.roll(core_z, 1, 1), pltpu.roll(outer_z, 1, 1)
+        core_left = jnp.where(first_col, outer_back, core_back)
+        outer_left = jnp.where(first_col, core_back, outer_back)
+        core_left, core_fore = jnp.where(near, core, core_left), jnp.where(far, core, core_z)
+        for zt, mid, down, z_left, z_right, z_pair in (
+            (0, core, core_down, core_left, core_fore, core_z),
+            (1, outer, outer_down, outer_left, outer_z, outer_z),
+        ):
+            below = jnp.where(plane == 0, mid, coef[0, zt, e - 1])
+            above = jnp.where(plane == plan.inset - 1, mid, coef[0, zt, e])
+            y_pair = jnp.where(okay, harmonic(mid, down), 0.0)
+            y_up = jnp.where(top, mid, pltpu.roll(y_pair, 1, 0))
+            y_down = jnp.where(bottom, mid, y_pair)
+            total = below + above + y_up + y_down + z_left + z_right
             valid = (maskv[zt] > 0.5) & okay
-            for f in range(6):
-                coef[f, zt, e] = jnp.where(valid, parts[f] / total, 0.0)
-            charge[zt, e] = jnp.where(valid, charge[zt, e] / total, 0.0)
-
-    def flux(old, zt, e, around):
-        _, up, down, left, right = around
-        value = charge[zt, e] + coef[0, zt, e] * old[zt, e - 1] + coef[1, zt, e] * old[zt, e + 1]
-        value = value + coef[2, zt, e] * up + coef[3, zt, e] * down
-        return value + coef[4, zt, e] * left + coef[5, zt, e] * right
-
-    def jacobi_wide(old, new):
-        @pl.loop(1, ext_x - 1)
+            coef[1, zt, e] = y_pair
+            coef[2, zt, e] = z_pair
+            coef[3, zt, e] = jnp.where(valid, 1.0 / total, 0.0)
+
+    def flux(old, e, outer_too):
+        core, outer = old[0, e], old[1, e]
+        core_z, outer_z = coef[2, 0, e], coef[2, 1, e]
+        core_r, outer_r = pltpu.roll(core, cz - 1, 1), pltpu.roll(outer, cz - 1, 1)
+        core_l, outer_l = pltpu.roll(core * core_z, 1, 1), pltpu.roll(outer * outer_z, 1, 1)
+        along = [jnp.where(last_col, outer_r, core_r) * core_z + jnp.where(first_col, outer_l, core_l)]
+        if outer_too:
+            along.append(jnp.where(last_col, core_r, outer_r) * outer_z + jnp.where(first_col, core_l, outer_l))
+        values = []
+        for zt, value in enumerate(along):
+            mid, y_pair = (core, outer)[zt], coef[1, zt, e]
+            value = value + charge[zt, e]
+            value = value + (coef[0, zt, e - 1] * old[zt, e - 1] + coef[0, zt, e] * old[zt, e + 1])
+            value = value + (y_pair * pltpu.roll(mid, ext_y - 1, 0) + pltpu.roll(y_pair * mid, 1, 0))
+            values.append(value * coef[3, zt, e])
+        return values
+
+    def jacobi_wide(old, new, low, high):
+        @pl.loop(low, high, unroll=True)
         def _(e):
-            for zt, around in enumerate(sides(old, e)):
-                new[zt, e] = flux(old, zt, e, around)
+            for zt, value in enumerate(flux(old, e, True)):
+                new[zt, e] = value
 
     def jacobi_core(old, new, slot):
-        @pl.loop(0, cx)
+        @pl.loop(0, cx, unroll=True)
         def _(k):
             e = k + WIDE
-            value = flux(old, 0, e, sides(old, e)[0])[0:cy]
+            value = flux(old, e, False)[0][0:cy]
             if slot is None:
                 last[k] = value
             else:
                 new[0, e, 0:cy] = value
                 send[slot, k] = value
 
-    for block in range(JACOBI // 2):
+    for block in range(JACOBI // 4):
+        final = block == JACOBI // 4 - 1
         if block > 0:
-            finish(5 + block)
-            assemble(5 + block, 0, put_init)
-        jacobi_wide(prs_a, prs_b)
-        final = block == JACOBI // 2 - 1
-        jacobi_core(prs_b, prs_a, None if final else plan.bases[6 + block])
+            finish(3 + block)
+            assemble(3 + block, 0, put_init)
+        for sweep in range(3):
+            old, new = (prs_a, prs_b) if sweep % 2 == 0 else (prs_b, prs_a)
+            jacobi_wide(old, new, sweep + 1, ext_x - sweep - 1)
+        jacobi_core(prs_b, prs_a, None if final else plan.bases[4 + block])
         if not final:
-            start(6 + block)
+            start(4 + block)
 
     def last_of(index, shift):
         low, high = plan.shifts[shift]
@@ -522,11 +564,13 @@
             jax.ShapeDtypeStruct(noise.shape, f32),
             jax.ShapeDtypeStruct(pressure_init.shape, f32),
         ),
-        in_specs=[pl.BlockSpec(memory_space=pltpu.SMEM)] + [pl.BlockSpec(memory_space=pltpu.VMEM)] * 4,
+        in_specs=[pl.BlockSpec(memory_space=pl.ANY)] * 5,
         out_specs=(pl.BlockSpec(memory_space=pltpu.VMEM),) * 2,
         scratch_shapes=[
             vmem(*block), vmem(*block), vmem(*block), vmem(*block), vmem(*block), vmem(*block),
-            vmem(6, *block), vmem(*block), vmem(*block), vmem(2, cy + 8, cz),
+            vmem(4, *block), vmem(*block), vmem(*block), vmem(2, cy + 8, cz),
+            vmem(*pressure_init.shape), vmem(*source.shape),
+            pltpu.SMEM(cuts.shape, jnp.int32), sems(5),
             vmem(total, cx, cy, cz), vmem(2, total, 8, cz),
             vmem(2, total, WIDE, cy, cz), vmem(2, total, cx, 8, cz),
             vmem(2, 2, total, WIDE, 8, cz), vmem(3, 3, 2, total, 8, cz),

time: 67.8 us -> 49.7 us (0.73)
  Pallas kernels: 61.3 us -> 43.2 us
    pallas_call x1, Pallas kernels: 61.3 us -> 43.2 us  [local(): pl.pallas_call(functools.partial(kernel, plan), out_shape=(jax.ShapeDtype...]
where the time goes in v2:
time: 49.7 us; the launch traced here: 49.5 us
  Pallas kernels  43.2 us (87%)
  local copies, waits for them, and re-layouts  5.61 us (11%)
  between operations  0.65 us (1%)
    pallas_call x1, Pallas kernels, local(): pl.pallas_call(functools.partial(kernel, plan), out_shape=(jax.ShapeDtype...  43.2 us
    unnamed x12, local copies, waits for them, and re-layouts  5.61 us

profile of v2, /device:TPU:0, one launch (start us, length us, event | category | flops | bytes accessed | tf_op | source)
XLA Modules:
  0.0 49.5 jit_solution(12162256681009462620)
XLA Ops:
  0.6 0.0 copy-start
  0.6 0.9 %copy-done = f32[10,32,128]{2,1,0:T(8,128)S(1)} copy-done((f32[10,32,128]{2,1,0:T(8,128)S(1)}, f32[10,32,128]{2,1,0:T(8,128)}, u32[]{:S(2)}) %copy-start) | copy-done | bytes 163864
  1.5 0.0 copy-start.1
  1.6 0.9 %copy-done.1 = f32[10,32,128]{2,1,0:T(8,128)S(1)} copy-done((f32[10,32,128]{2,1,0:T(8,128)S(1)}, f32[10,32,128]{2,1,0:T(8,128)}, u32[]{:S(2)}) %copy-start.1) | copy-done | bytes 163864
  2.5 0.0 copy-start.2
  2.5 0.9 %copy-done.2 = f32[8,32,128]{2,1,0:T(8,128)S(1)} copy-done((f32[8,32,128]{2,1,0:T(8,128)S(1)}, f32[8,32,128]{2,1,0:T(8,128)}, u32[]{:S(2)}) %copy-start.2) | copy-done | bytes 131096
  3.4 0.0 copy-start.3
  3.4 0.9 %copy-done.3 = f32[8,32,128]{2,1,0:T(8,128)S(1)} copy-done((f32[8,32,128]{2,1,0:T(8,128)S(1)}, f32[8,32,128]{2,1,0:T(8,128)}, u32[]{:S(2)}) %copy-start.3) | copy-done | bytes 131096
  4.3 0.0 copy-start.4
  4.3 0.7 %copy-done.4 = s32[6]{0:T(128)S(1)} copy-done((s32[6]{0:T(128)S(1)}, s32[6]{0:T(128)}, u32[]{:S(2)}) %copy-start.4) | copy-done | bytes 48
  4.9 43.2 %sweeps.1 = (f32[8,32,128]{2,1,0:T(8,128)S(1)}, f32[10,32,128]{2,1,0:T(8,128)S(1)}) custom-call(s32[6]{0:T(128)S(1)} %copy-done.4, f32[8,32,128]{2,1,0:T(8,128)S(1)} %copy-done.2, f32[8,32,128]{2,1,0:T(8,128)S(1)} %copy-done.3, f32[10,32,128]{2,1,0:T(8,128)S(1)} %copy-done, f32[10,32,128]{2,1,0:T(8,128)S(1)} %copy-done.1), custom_call_target="tpu_custom_call" | custom-call | flops 30000000 | bytes 1000000 | tf_op jit(solution)/shard_map/sweeps/pallas_call | solution.py:561
  48.1 0.7 %copy.9 = f32[8,32,128]{2,1,0:T(8,128)} copy(f32[8,32,128]{2,1,0:T(8,128)S(1)} %get-tuple-element.4) | data formatting | bytes 262144
  48.8 0.7 %copy.10 = f32[10,32,128]{2,1,0:T(8,128)} copy(f32[10,32,128]{2,1,0:T(8,128)S(1)} %get-tuple-element.5) | data formatting | bytes 327680
Async XLA Ops:
  0.6 0.9 %copy-start = (f32[10,32,128]{2,1,0:T(8,128)S(1)}, f32[10,32,128]{2,1,0:T(8,128)}, u32[]{:S(2)}) copy-start(f32[10,32,128]{2,1,0:T(8,128)} %init_hbm.1) | copy-start | bytes 491524
  1.5 0.9 %copy-start.1 = (f32[10,32,128]{2,1,0:T(8,128)S(1)}, f32[10,32,128]{2,1,0:T(8,128)}, u32[]{:S(2)}) copy-start(f32[10,32,128]{2,1,0:T(8,128)} %source_hbm.1) | copy-start | bytes 491524
  2.5 0.9 %copy-start.2 = (f32[8,32,128]{2,1,0:T(8,128)S(1)}, f32[8,32,128]{2,1,0:T(8,128)}, u32[]{:S(2)}) copy-start(f32[8,32,128]{2,1,0:T(8,128)} %noise_hbm.1) | copy-start | bytes 393220
  3.4 0.9 %copy-start.3 = (f32[8,32,128]{2,1,0:T(8,128)S(1)}, f32[8,32,128]{2,1,0:T(8,128)}, u32[]{:S(2)}) copy-start(f32[8,32,128]{2,1,0:T(8,128)} %kappa_hbm.1) | copy-start | bytes 393220
  4.3 0.7 %copy-start.4 = (s32[6]{0:T(128)S(1)}, s32[6]{0:T(128)}, u32[]{:S(2)}) copy-start(s32[6]{0:T(128)} %cuts_hbm.1) | copy-start | bytes 76

commit v3 on v2

--- a/solution.py
+++ b/solution.py
@@ -68,7 +68,7 @@
     plan,
     cuts_hbm, noise_hbm, kappa_hbm, init_hbm, source_hbm,
     field_ref, pressure_ref,
-    dir_a, dir_b, resid, kap, prs_a, prs_b, coef, charge, perm, maskv,
+    dirs, resid, kap, press, coef, charge, perm, maskv,
     init_in, source_in, cuts_in, load_sem,
     send, packed, land_x, land_y, land_xy, land_p,
     move_out, move_in, last, landed,
@@ -119,15 +119,27 @@
 
     pl.semaphore_wait(barrier, expected)
 
+    dir_l, prs_l = [dirs.at[i] for i in range(4)], [press.at[i] for i in range(4)]
+    dir_a, prs_a = dir_l[0], prs_l[0]
     lane = lax.broadcasted_iota(jnp.int32, (8, cz), 1)
     row8 = lax.broadcasted_iota(jnp.int32, (8, cz), 0)
 
     def offsets_of(width):
         return [(i, o) for i, o in enumerate(OFFSETS) if sum(map(abs, o)) <= width]
 
-    def copy_of(rnd, index, o):
+    def copies_of(rnd):
+        n, w = plan.rounds[rnd]
+        listed = [(i, o, 0) for i, o in offsets_of(w)]
+        if n > 1:
+            extra = [o for o in OFFSETS if o[1] == 0 and o[2] == 0]
+            listed = [(len(OFFSETS) + i, o, 1) for i, o in enumerate(extra)] + listed
+        return sorted(listed, key=lambda c: (c[1][2] != 0, c[1][0] == 0 or c[1][1] != 0, c[2]))
+
+    def copy_of(rnd, index, o, a):
         n, w = plan.rounds[rnd]
         arrays = pl.ds(plan.bases[rnd], n)
+        if o[0] != 0 and o[1] == 0 and o[2] == 0:
+            w, arrays = w - a, pl.ds(plan.bases[rnd] + a, 1)
         planes = {0: pl.ds(0, cx), 1: pl.ds(cx - w, w), -1: pl.ds(0, w)}[o[0]]
         rows = {0: pl.ds(0, cy), 1: pl.ds(cy - 8, 8), -1: pl.ds(0, 8)}[o[1]]
         fx, fy = (0 if o[0] > 0 else 1), (0 if o[1] > 0 else 1)
@@ -153,14 +165,14 @@
     def start(rnd):
         n, w = plan.rounds[rnd]
 
-        def begin(index, o):
+        def begin(index, o, a):
             @pl.when(has[o])
             def _():
-                copy_of(rnd, index, o).start()
-
-        for index, o in offsets_of(w):
+                copy_of(rnd, index, o, a).start()
+
+        for index, o, a in copies_of(rnd):
             if o[2] == 0:
-                begin(index, o)
+                begin(index, o, a)
         for a in range(n):
             slot = plan.bases[rnd] + a
             low = jnp.zeros((8, cz), jnp.float32)
@@ -176,31 +188,30 @@
                     )
             packed[0, slot] = low
             packed[1, slot] = high
-        for index, o in offsets_of(w):
+        for index, o, a in copies_of(rnd):
             if o[2] != 0:
-                begin(index, o)
-
-    def finish(rnd):
-        n, w = plan.rounds[rnd]
-        for index, o in offsets_of(w):
-            back = tuple(-v for v in o)
-
-            @pl.when(has[back])
-            def _(index=index, o=o):
-                copy_of(rnd, index, o).wait_recv()
-
-        for index, o in offsets_of(w):
+                begin(index, o, a)
+
+    def finish(rnd, beside):
+        for index, o, a in copies_of(rnd):
+            if (o[0] == 0) == beside:
+                @pl.when(has[tuple(-v for v in o)])
+                def _(index=index, o=o, a=a):
+                    copy_of(rnd, index, o, a).wait_recv()
+
+    def let_go(rnd):
+        for index, o, a in copies_of(rnd):
             @pl.when(has[o])
-            def _(index=index, o=o):
-                copy_of(rnd, index, o).wait_send()
-
-    def assemble(rnd, a, put, fill=0.0):
+            def _(index=index, o=o, a=a):
+                copy_of(rnd, index, o, a).wait_send()
+
+    def assemble(rnd, a, put, beside, fill=0.0):
         n, w = plan.rounds[rnd]
         slot = plan.bases[rnd] + a
         blank = jnp.full((8, cz), fill, jnp.float32)
         arrived = {}
         for o in OFFSETS:
-            if o[2] != 0 and sum(map(abs, o)) <= w:
+            if o[2] != 0 and sum(map(abs, o)) <= w and (o[0] == 0) == beside:
                 side = 0 if o[2] > 0 else 1
                 arrived[o] = jnp.where(has[o], land_p[1 + o[0], 1 + o[1], side, slot], blank)
 
@@ -222,28 +233,25 @@
                 put(1, plane, 8 * j, unpack(dx, 0, k, j))
             put(1, plane, cy, between(unpack(dx, 1, k, 0), unpack(dx, -1, k, tiles_y - 1)))
 
-        for k in range(cx):
+        for k in range(cx) if beside else ():
             after = jnp.where(has[0, 1, 0], land_y[1, slot, k], blank)
             before = jnp.where(has[0, -1, 0], land_y[0, slot, k], blank)
             put(0, WIDE + k, cy, between(after, before))
             columns(0, k, WIDE + k)
-        for dx in (-1, 1):
+        wide = w - a
+        for dx in () if beside else (-1, 1):
             fx = 0 if dx < 0 else 1
-            for q in range(w):
-                plane = WIDE - w + q if dx < 0 else WIDE + cx + q
-                k = cx - w + q if dx < 0 else q
+            for q in range(wide):
+                plane = WIDE - wide + q if dx < 0 else WIDE + cx + q
+                k = cx - wide + q if dx < 0 else q
+                i = q + a if dx < 0 else q
                 big = jnp.where(has[dx, 0, 0], land_x[fx, slot, q], jnp.full((cy, cz), fill, jnp.float32))
                 for j in range(tiles_y):
                     put(0, plane, 8 * j, big[8 * j : 8 * j + 8])
-                if w > 1:
-                    after = jnp.where(has[dx, 1, 0], land_xy[fx, 1, slot, q], blank)
-                    before = jnp.where(has[dx, -1, 0], land_xy[fx, 0, slot, q], blank)
-                    put(0, plane, cy, between(after, before))
-                    columns(dx, k, plane)
-                else:
-                    put(0, plane, cy, blank)
-                    for j in range(tiles_y + 1):
-                        put(1, plane, 8 * j, blank)
+                after = jnp.where(has[dx, 1, 0], land_xy[fx, 1, slot, i], blank)
+                before = jnp.where(has[dx, -1, 0], land_xy[fx, 0, slot, i], blank)
+                put(0, plane, cy, between(after, before))
+                columns(dx, k, plane)
 
     loads[0].wait()
     loads[1].wait()
@@ -320,9 +328,18 @@
         return (at >= 0) & (at < plan.size[0] * cx)
 
     def planes_of(low, high):
-        for first, end, own in ((low, WIDE, False), (WIDE, WIDE + cx, True), (WIDE + cx, high, False)):
+        for first, end, own in ((0, WIDE, False), (WIDE, WIDE + cx, True), (WIDE + cx, ext_x, False)):
+            first, end = max(first, low), min(end, high)
             if first < end:
                 yield first, end, own
+
+    def parts(step, width, beside):
+        low, high = WIDE - width + step + 1, WIDE + cx + width - step - 1
+        inner_low, inner_high = WIDE + 1 + step, WIDE + cx - 1 - step
+        inner_low = min(inner_low, inner_high)
+        if beside:
+            return [(inner_low, inner_high)]
+        return [(low, inner_low), (inner_high, high)]
 
     def cheb_wide(old, new, weight, low, high):
         for first, end, own in planes_of(low, high):
@@ -339,10 +356,10 @@
                     if own and zt == 0:
                         field_ref[e - WIDE] = field_ref[e - WIDE] + value[0:cy]
 
-    def cheb_core(old, new, weight, slot):
-        @pl.loop(0, cx, unroll=True)
-        def _(k):
-            e = k + WIDE
+    def cheb_core(old, new, weight, slot, low, high):
+        @pl.loop(low, high, unroll=True)
+        def _(e):
+            k = e - WIDE
             mid, up, down, left, right = sides(old, e)[0]
             beside = old[0, e - 1] + old[0, e + 1] + (up + down) + (left + right)
             rest = (resid[0, e] - (kap[0, e] * mid - beside))[0:cy]
@@ -359,7 +376,16 @@
                 send[slot, k] = value
                 send[slot + 1, k] = rest
 
-    finish(0)
+    def cheb_block(beside, first, count, slot):
+        for step in range(count):
+            for low, high in parts(step, count, beside):
+                if low >= high:
+                    continue
+                weight = weights[first + step]
+                if step < count - 1:
+                    cheb_wide(dir_l[step], dir_l[step + 1], weight, low, high)
+                else:
+                    cheb_core(dir_l[step], dir_a, weight, slot, low, high)
 
     def put_noise(zt, e, r, value):
         resid[zt, e, r : r + 8] = value
@@ -368,12 +394,11 @@
     def put_kappa(zt, e, r, value):
         kap[zt, e, r : r + 8] = value + 6.0
 
-    assemble(0, 0, put_noise)
-    assemble(0, 1, put_kappa)
-    for sweep in range(3):
-        old, new = (dir_a, dir_b) if sweep % 2 == 0 else (dir_b, dir_a)
-        cheb_wide(old, new, weights[sweep], sweep + 1, ext_x - sweep - 1)
-    cheb_core(dir_b, dir_a, weights[3], plan.bases[1])
+    for beside in (True, False):
+        finish(0, beside)
+        assemble(0, 0, put_noise, beside)
+        assemble(0, 1, put_kappa, beside)
+        cheb_block(beside, 0, 4, plan.bases[1])
     start(1)
 
     for index, shift in enumerate(plan.moves):
@@ -397,15 +422,13 @@
     def put_resid(zt, e, r, value):
         resid[zt, e, r : r + 8] = value
 
-    finish(1)
-    assemble(1, 0, put_dir)
-    assemble(1, 1, put_resid)
-    cheb_wide(dir_a, dir_b, weights[4], 2, ext_x - 2)
-    cheb_wide(dir_b, dir_a, weights[5], 3, ext_x - 3)
-    cheb_core(dir_a, None, weights[6], None)
+    for beside in (True, False):
+        finish(1, beside)
+        assemble(1, 0, put_dir, beside)
+        assemble(1, 1, put_resid, beside)
+        cheb_block(beside, 4, 3, None)
     start(3)
 
-    finish(2)
 
     def put_init(zt, e, r, value):
         prs_a[zt, e, r : r + 8] = value
@@ -413,18 +436,18 @@
     def put_charge(zt, e, r, value):
         charge[zt, e, r : r + 8] = value
 
-    assemble(2, 0, put_init)
-    assemble(2, 1, put_charge)
+    for beside in (True, False):
+        finish(2, beside)
+        assemble(2, 0, put_init, beside)
+        assemble(2, 1, put_charge, beside)
     for k in range(cx):
         prs_a[0, WIDE + k, 0:cy] = send[slot_q, k]
         charge[0, WIDE + k, 0:cy] = send[slot_q + 1, k]
 
-    finish(3)
 
     def put_perm(zt, e, r, value):
         perm[zt, e, r : r + 8] = value
 
-    assemble(3, 0, put_perm, fill=1.0)
 
     top = (row == 0) & (me[1] == 0)
     bottom = (row == cy - 1) & (me[1] == plan.size[1] - 1)
@@ -434,15 +457,13 @@
     def harmonic(own, other):
         return 2.0 * own * other / (own + other)
 
-    @pl.loop(0, ext_x - 1, unroll=True)
-    def _(e):
+    def couple_x(e):
         plane = me[0] * cx - WIDE + e - inset_begin
         pair = (plane >= 0) & (plane < plan.inset - 1)
         for zt in range(2):
             coef[0, zt, e] = jnp.where(pair, harmonic(perm[zt, e], perm[zt, e + 1]), 0.0)
 
-    @pl.loop(1, ext_x - 1, unroll=True)
-    def _(e):
+    def couple(e):
         plane = me[0] * cx - WIDE + e - inset_begin
         okay = (plane >= 0) & (plane < plan.inset)
         (core, _, core_down, _, core_right), (outer, _, outer_down, _, outer_right) = sides(perm, e)
@@ -490,10 +511,10 @@
             for zt, value in enumerate(flux(old, e, True)):
                 new[zt, e] = value
 
-    def jacobi_core(old, new, slot):
-        @pl.loop(0, cx, unroll=True)
-        def _(k):
-            e = k + WIDE
+    def jacobi_core(old, new, slot, low, high):
+        @pl.loop(low, high, unroll=True)
+        def _(e):
+            k = e - WIDE
             value = flux(old, e, False)[0][0:cy]
             if slot is None:
                 last[k] = value
@@ -501,17 +522,32 @@
                 new[0, e, 0:cy] = value
                 send[slot, k] = value
 
-    for block in range(JACOBI // 4):
-        final = block == JACOBI // 4 - 1
-        if block > 0:
-            finish(3 + block)
-            assemble(3 + block, 0, put_init)
-        for sweep in range(3):
-            old, new = (prs_a, prs_b) if sweep % 2 == 0 else (prs_b, prs_a)
-            jacobi_wide(old, new, sweep + 1, ext_x - sweep - 1)
-        jacobi_core(prs_b, prs_a, None if final else plan.bases[4 + block])
-        if not final:
-            start(4 + block)
+    def jacobi_block(beside, count, slot):
+        for step in range(count):
+            for low, high in parts(step, count, beside):
+                if low >= high:
+                    continue
+                if step < count - 1:
+                    jacobi_wide(prs_l[step], prs_l[step + 1], low, high)
+                else:
+                    jacobi_core(prs_l[step], prs_a, slot, low, high)
+
+    def over(ranges, body):
+        for low, high in ranges:
+            pl.loop(low, high, unroll=True)(body)
+
+    inner, end = WIDE + cx - 1, ext_x - 1
+    for beside in (True, False):
+        finish(3, beside)
+        assemble(3, 0, put_perm, beside, fill=1.0)
+        over([(WIDE, inner)] if beside else [(0, WIDE), (inner, end)], couple_x)
+        over([(WIDE + 1, inner)] if beside else [(1, WIDE + 1), (inner, end)], couple)
+        jacobi_block(beside, 4, plan.bases[4])
+    start(4)
+    for beside in (True, False):
+        finish(4, beside)
+        assemble(4, 0, put_init, beside)
+        jacobi_block(beside, 4, None)
 
     def last_of(index, shift):
         low, high = plan.shifts[shift]
@@ -546,6 +582,9 @@
         @pl.when(has[-shift, 0, 0])
         def _(index=index, shift=shift):
             last_of(index, shift).wait_send()
+
+    for rnd in range(len(plan.rounds)):
+        let_go(rnd)
 
 
 def local(mesh, noise, kappa_sq, cuts, pressure_init, source):
@@ -567,7 +606,7 @@
         in_specs=[pl.BlockSpec(memory_space=pl.ANY)] * 5,
         out_specs=(pl.BlockSpec(memory_space=pltpu.VMEM),) * 2,
         scratch_shapes=[
-            vmem(*block), vmem(*block), vmem(*block), vmem(*block), vmem(*block), vmem(*block),
+            vmem(4, *block), vmem(*block), vmem(*block), vmem(4, *block),
             vmem(4, *block), vmem(*block), vmem(*block), vmem(2, cy + 8, cz),
             vmem(*pressure_init.shape), vmem(*source.shape),
             pltpu.SMEM(cuts.shape, jnp.int32), sems(5),
@@ -576,11 +615,11 @@
             vmem(2, 2, total, WIDE, 8, cz), vmem(3, 3, 2, total, 8, cz),
             vmem(moves, 2, cx, cy, cz), vmem(moves, 2, cx, cy, cz),
             vmem(cx, cy, cz), vmem((plan.highest - plan.lowest + 1) * cx, cy, cz),
-            sems(len(plan.rounds), len(OFFSETS)), sems(len(plan.rounds), len(OFFSETS)),
+            sems(len(plan.rounds), len(OFFSETS) + 2), sems(len(plan.rounds), len(OFFSETS) + 2),
             sems(moves), sems(moves), sems(moves), sems(moves),
         ],
         compiler_params=pltpu.CompilerParams(
-            collective_id=0, has_side_effects=True, vmem_limit_bytes=48 * 1024 * 1024
+            collective_id=0, has_side_effects=True, vmem_limit_bytes=64 * 1024 * 1024
         ),
         cost_estimate=pl.CostEstimate(flops=30_000_000, bytes_accessed=1_000_000, transcendentals=32768),
         name="sweeps",

time: 49.7 us -> 43.2 us (0.87)
  local copies, waits for them, and re-layouts: 5.61 us -> 2.28 us
  Pallas kernels: 43.2 us -> 40.1 us
    unnamed x12 -> x4, local copies, waits for them, and re-layouts: 5.61 us -> 2.28 us
    pallas_call x1, Pallas kernels: 43.2 us -> 40.1 us  [local(): pl.pallas_call(functools.partial(kernel, plan), out_shape=(jax.ShapeDtype...]
where the time goes in v3:
time: 43.2 us; the launch traced here: 43.1 us
  Pallas kernels  40.1 us (93%)
  local copies, waits for them, and re-layouts  2.28 us (5%)
  between operations  0.65 us (2%)
    pallas_call x1, Pallas kernels, local(): pl.pallas_call(functools.partial(kernel, plan), out_shape=(jax.ShapeDtype...  40.1 us
    unnamed x4, local copies, waits for them, and re-layouts  2.28 us

profile of v3, /device:TPU:0, one launch (start us, length us, event | category | flops | bytes accessed | tf_op | source)
XLA Modules:
  0.0 43.1 jit_solution(366871372548885999)
XLA Ops:
  0.6 40.1 %sweeps.1 = (f32[8,32,128]{2,1,0:T(8,128)}, f32[10,32,128]{2,1,0:T(8,128)}) custom-call(s32[6]{0:T(128)} %cuts_hbm.1, f32[8,32,128]{2,1,0:T(8,128)} %noise_hbm.1, f32[8,32,128]{2,1,0:T(8,128)} %kappa_hbm.1, f32[10,32,128]{2,1,0:T(8,128)} %init_hbm.1, f32[10,32,128]{2,1,0:T(8,128)} %source_hbm.1), custom_call_target="tpu_custom_call" | custom-call | flops 30000000 | bytes 1000000 | tf_op jit(solution)/shard_map/sweeps/pallas_call | solution.py:600
  40.8 0.0 copy-start
  40.8 1.6 %copy.9 = f32[8,32,128]{2,1,0:T(8,128)} copy(f32[8,32,128]{2,1,0:T(8,128)} %get-tuple-element.4) | data formatting | bytes 262144
  42.4 0.0 copy-done
  42.4 0.7 %copy.10 = f32[10,32,128]{2,1,0:T(8,128)} copy(f32[10,32,128]{2,1,0:T(8,128)S(1)} %copy-done) | data formatting | bytes 327680
Async XLA Ops:
  40.8 1.6 %copy-start = (f32[10,32,128]{2,1,0:T(8,128)S(1)}, f32[10,32,128]{2,1,0:T(8,128)}, u32[]{:S(2)}) copy-start(f32[10,32,128]{2,1,0:T(8,128)} %get-tuple-element.5) | copy-start | bytes 491524

commit v4 on v3

--- a/solution.py
+++ b/solution.py
@@ -117,7 +117,6 @@
         def _(o=o):
             pl.semaphore_signal(barrier, inc=1, device_id=device(o), device_id_type=MESH)
 
-    pl.semaphore_wait(barrier, expected)
 
     dir_l, prs_l = [dirs.at[i] for i in range(4)], [press.at[i] for i in range(4)]
     dir_a, prs_a = dir_l[0], prs_l[0]
@@ -162,35 +161,38 @@
             device_id=device(o), device_id_type=MESH,
         )
 
-    def start(rnd):
+    def issue(rnd, chosen):
+        for index, o, a in copies_of(rnd):
+            if chosen(o):
+                @pl.when(has[o])
+                def _(index=index, o=o, a=a):
+                    copy_of(rnd, index, o, a).start()
+
+    def pack(rnd):
         n, w = plan.rounds[rnd]
-
-        def begin(index, o, a):
-            @pl.when(has[o])
-            def _():
-                copy_of(rnd, index, o, a).start()
-
-        for index, o, a in copies_of(rnd):
-            if o[2] == 0:
-                begin(index, o, a)
         for a in range(n):
             slot = plan.bases[rnd] + a
-            low = jnp.zeros((8, cz), jnp.float32)
-            high = jnp.zeros((8, cz), jnp.float32)
+            low = high = None
             for k in range(cx):
                 for j in range(tiles_y):
                     by = (j * cx + k) * w
                     value = send[slot, k, 8 * j : 8 * j + 8]
-                    low = jnp.where((lane >= by) & (lane < by + w), pltpu.roll(value, by, 1), low)
-                    back = (cz - by) % cz
-                    high = jnp.where(
-                        (lane >= cz - w - by) & (lane < cz - by), pltpu.roll(value, back, 1), high
-                    )
+                    to_low = jnp.where(lane < w, value, 0.0)
+                    to_high = jnp.where(lane >= cz - w, value, 0.0)
+                    if by:
+                        to_low = low + pltpu.roll(to_low, by, 1)
+                        to_high = high + pltpu.roll(to_high, cz - by, 1)
+                    low, high = to_low, to_high
             packed[0, slot] = low
             packed[1, slot] = high
-        for index, o, a in copies_of(rnd):
-            if o[2] != 0:
-                begin(index, o, a)
+
+    def start(rnd, ready=False):
+        issue(rnd, lambda o: o[0] == 0 and o[2] == 0)
+        if not ready:
+            pack(rnd)
+        issue(rnd, lambda o: o[0] == 0 and o[2] != 0)
+        issue(rnd, lambda o: o[0] != 0 and o[2] == 0)
+        issue(rnd, lambda o: o[0] != 0 and o[2] != 0)
 
     def finish(rnd, beside):
         for index, o, a in copies_of(rnd):
@@ -255,7 +257,9 @@
 
     loads[0].wait()
     loads[1].wait()
-    start(0)
+    pack(0)
+    pl.semaphore_wait(barrier, expected)
+    start(0, ready=True)
     for load in loads[2:]:
         load.wait()
 

time: 43.2 us -> 43.6 us (level)
  no operation moved by 1% of the time
where the time goes in v4:
time: 43.6 us; the launch traced here: 43.5 us
  Pallas kernels  40.5 us (93%)
  local copies, waits for them, and re-layouts  2.28 us (5%)
  between operations  0.65 us (1%)
    pallas_call x1, Pallas kernels, local(): pl.pallas_call(functools.partial(kernel, plan), out_shape=(jax.ShapeDtype...  40.5 us
    unnamed x4, local copies, waits for them, and re-layouts  2.28 us

profile of v4, /device:TPU:0, one launch (start us, length us, event | category | flops | bytes accessed | tf_op | source)
XLA Modules:
  0.0 43.5 jit_solution(3741264531982565412)
XLA Ops:
  0.6 40.5 %sweeps.1 = (f32[8,32,128]{2,1,0:T(8,128)}, f32[10,32,128]{2,1,0:T(8,128)}) custom-call(s32[6]{0:T(128)} %cuts_hbm.1, f32[8,32,128]{2,1,0:T(8,128)} %noise_hbm.1, f32[8,32,128]{2,1,0:T(8,128)} %kappa_hbm.1, f32[10,32,128]{2,1,0:T(8,128)} %init_hbm.1, f32[10,32,128]{2,1,0:T(8,128)} %source_hbm.1), custom_call_target="tpu_custom_call" | custom-call | flops 30000000 | bytes 1000000 | tf_op jit(solution)/shard_map/sweeps/pallas_call | solution.py:604
  41.2 0.0 copy-start
  41.2 1.6 %copy.9 = f32[8,32,128]{2,1,0:T(8,128)} copy(f32[8,32,128]{2,1,0:T(8,128)} %get-tuple-element.4) | data formatting | bytes 262144
  42.8 0.0 copy-done
  42.8 0.7 %copy.10 = f32[10,32,128]{2,1,0:T(8,128)} copy(f32[10,32,128]{2,1,0:T(8,128)S(1)} %copy-done) | data formatting | bytes 327680
Async XLA Ops:
  41.2 1.6 %copy-start = (f32[10,32,128]{2,1,0:T(8,128)S(1)}, f32[10,32,128]{2,1,0:T(8,128)}, u32[]{:S(2)}) copy-start(f32[10,32,128]{2,1,0:T(8,128)} %get-tuple-element.5) | copy-start | bytes 491524

commit v5 on v4

--- a/solution.py
+++ b/solution.py
@@ -187,12 +187,10 @@
             packed[1, slot] = high
 
     def start(rnd, ready=False):
-        issue(rnd, lambda o: o[0] == 0 and o[2] == 0)
+        issue(rnd, lambda o: o[2] == 0)
         if not ready:
             pack(rnd)
-        issue(rnd, lambda o: o[0] == 0 and o[2] != 0)
-        issue(rnd, lambda o: o[0] != 0 and o[2] == 0)
-        issue(rnd, lambda o: o[0] != 0 and o[2] != 0)
+        issue(rnd, lambda o: o[2] != 0)
 
     def finish(rnd, beside):
         for index, o, a in copies_of(rnd):
@@ -347,7 +345,7 @@
 
     def cheb_wide(old, new, weight, low, high):
         for first, end, own in planes_of(low, high):
-            @pl.loop(first, end, unroll=True)
+            @pl.loop(first, end, unroll=2)
             def _(e, own=own):
                 okay = jnp.where(inside(e), 1.0, 0.0)
                 for zt, (mid, up, down, left, right) in enumerate(sides(old, e)):
@@ -361,7 +359,7 @@
                         field_ref[e - WIDE] = field_ref[e - WIDE] + value[0:cy]
 
     def cheb_core(old, new, weight, slot, low, high):
-        @pl.loop(low, high, unroll=True)
+        @pl.loop(low, high, unroll=2)
         def _(e):
             k = e - WIDE
             mid, up, down, left, right = sides(old, e)[0]
@@ -510,13 +508,13 @@
         return values
 
     def jacobi_wide(old, new, low, high):
-        @pl.loop(low, high, unroll=True)
+        @pl.loop(low, high, unroll=2)
         def _(e):
             for zt, value in enumerate(flux(old, e, True)):
                 new[zt, e] = value
 
     def jacobi_core(old, new, slot, low, high):
-        @pl.loop(low, high, unroll=True)
+        @pl.loop(low, high, unroll=2)
         def _(e):
             k = e - WIDE
             value = flux(old, e, False)[0][0:cy]
@@ -538,7 +536,7 @@
 
     def over(ranges, body):
         for low, high in ranges:
-            pl.loop(low, high, unroll=True)(body)
+            pl.loop(low, high, unroll=2)(body)
 
     inner, end = WIDE + cx - 1, ext_x - 1
     for beside in (True, False):

time: 43.6 us -> 46 us (1.055)
  Pallas kernels: 40.5 us -> 42.9 us
    pallas_call x1, Pallas kernels: 40.5 us -> 42.9 us  [local(): pl.pallas_call(functools.partial(kernel, plan), out_shape=(jax.ShapeDtype...]
where the time goes in v5:
time: 46 us; the launch traced here: 45.8 us
  Pallas kernels  42.9 us (93%)
  local copies, waits for them, and re-layouts  2.28 us (5%)
  between operations  0.65 us (1%)
    pallas_call x1, Pallas kernels, local(): pl.pallas_call(functools.partial(kernel, plan), out_shape=(jax.ShapeDtype...  42.9 us
    unnamed x4, local copies, waits for them, and re-layouts  2.28 us

profile of v5, /device:TPU:0, one launch (start us, length us, event | category | flops | bytes accessed | tf_op | source)
XLA Modules:
  0.0 45.8 jit_solution(17111523597121926032)
XLA Ops:
  0.6 42.9 %sweeps.1 = (f32[8,32,128]{2,1,0:T(8,128)}, f32[10,32,128]{2,1,0:T(8,128)}) custom-call(s32[6]{0:T(128)} %cuts_hbm.1, f32[8,32,128]{2,1,0:T(8,128)} %noise_hbm.1, f32[8,32,128]{2,1,0:T(8,128)} %kappa_hbm.1, f32[10,32,128]{2,1,0:T(8,128)} %init_hbm.1, f32[10,32,128]{2,1,0:T(8,128)} %source_hbm.1), custom_call_target="tpu_custom_call" | custom-call | flops 30000000 | bytes 1000000 | tf_op jit(solution)/shard_map/sweeps/pallas_call | solution.py:602
  43.6 0.0 copy-start
  43.6 1.6 %copy.9 = f32[8,32,128]{2,1,0:T(8,128)} copy(f32[8,32,128]{2,1,0:T(8,128)} %get-tuple-element.4) | data formatting | bytes 262144
  45.2 0.0 copy-done
  45.2 0.7 %copy.10 = f32[10,32,128]{2,1,0:T(8,128)} copy(f32[10,32,128]{2,1,0:T(8,128)S(1)} %copy-done) | data formatting | bytes 327680
Async XLA Ops:
  43.6 1.6 %copy-start = (f32[10,32,128]{2,1,0:T(8,128)S(1)}, f32[10,32,128]{2,1,0:T(8,128)}, u32[]{:S(2)}) copy-start(f32[10,32,128]{2,1,0:T(8,128)} %get-tuple-element.5) | copy-start | bytes 491524
